TPU v7x, 32 devices: a whole 2x2x4 slice. The times are simulated.
32 devices in a mesh: dp: 4 (over z), ctx: 2 (over x), tensor: 4 (over y, core).
Axes of the slice: x: 2, y: 2, z: 4, core: 2. Of those that a mesh axis runs over, the one named last changes fastest.
Arguments:
- inputs: bfloat16 [8, 1024, 768], P('dp', 'ctx'), may hold values from -6 to 6
- lengths: int32 [8], P('dp'), may hold values from 256 to 1024, as said below
- expert_ids: int32 [8, 1024], P('dp', 'ctx'), may hold values from 0 to 3, as said below
- slot_rows: int32 [8, 2, 4, 256], P('dp', 'ctx'), may hold values from 0 to 512, as said below
- attn_gain: bfloat16 [768], P(('dp', 'ctx')), may hold values from 0.5 to 1.5
- qkv_weight: bfloat16 [3, 768, 768], P(None, ('dp', 'ctx'), 'tensor'), may hold values from -0.21875 to 0.21875
- out_weight: bfloat16 [768, 768], P('tensor', ('dp', 'ctx')), may hold values from -1.75 to 1.75
- position_bias: float32 [32, 12], P(None, 'tensor'), may hold values from -3 to 3
- ffn_gain: bfloat16 [768], P(('dp', 'ctx')), may hold values from 0.5 to 1.5
- router_weight: bfloat16 [768, 4], P(('dp', 'ctx')), may hold values from -0.125 to 0.125
- up_weight: bfloat16 [4, 768, 3072], P(None, ('dp', 'ctx'), 'tensor'), may hold values from -0.21875 to 0.21875
- down_weight: bfloat16 [4, 3072, 768], P(None, 'tensor', ('dp', 'ctx')), may hold values from -0.875 to 0.875
- cotangent: bfloat16 [8, 1024, 768], P('dp', 'ctx'), may hold values from -6 to 6
Outputs:
- outputs: bfloat16 [8, 1024, 768], P('dp', 'ctx')
- input_grad: bfloat16 [8, 1024, 768], P('dp', 'ctx')
- attn_gain_grad: float32 [768], P(('dp', 'ctx'))
- qkv_grad: float32 [3, 768, 768], P(None, ('dp', 'ctx'), 'tensor')
- out_proj_grad: float32 [768, 768], P('tensor', ('dp', 'ctx'))
- bias_table_grad: float32 [32, 12], P(None, 'tensor')
- ffn_gain_grad: float32 [768], P(('dp', 'ctx'))
- router_grad: float32 [768, 4], P(('dp', 'ctx'))
- up_grad: float32 [4, 768, 3072], P(None, ('dp', 'ctx'), 'tensor')
- down_grad: float32 [4, 3072, 768], P(None, 'tensor', ('dp', 'ctx'))
Inputs may be any that keep to these rules, and one draw needn't show every extreme that they name: `lengths`: in each group of 2 sequences that one index of dp holds, one has length 1024; some sequence has length 256. `expert_ids`: position t's expert is the expert in whose slots of t's segment it stands in slot_rows. `slot_rows`: entries are positions within the segment; 512 marks an empty slot. Every position of a segment stands in exactly one slot, and in every segment one expert fills all 256 of its slots.
All inputs are finite; a program needn't handle non-finite values.
Results may differ from a plain program's by a relative error of at most 0.025.
Values may be sent and summed in bfloat16 or wider, within the bound.
A program may use at most 384 MiB of HBM per device.

v0:
```python
import functools

import jax
import jax.numpy as jnp
import numpy as np
from jax import lax
from jax.experimental import pallas as pl
from jax.experimental.pallas import tpu as pltpu
from jax.sharding import PartitionSpec as P

BUCKETS = 32
MESH = pl.DeviceIdType.MESH
BF = jnp.bfloat16
F32 = jnp.float32


bucket_edges = np.ceil(16.0 * 8.0 ** (np.arange(1, 16) / 16.0)).astype(np.int32)
bucket_starts = [int(n) for n in range(17)] + [int(n) for n in bucket_edges]


QT = 256
BAND = 128
C0 = float(np.sqrt(2.0 / np.pi))
C1 = 0.044715


def mm(a, b):
    return jnp.dot(a, b, preferred_element_type=F32)


def mm_nt(a, b):
    return lax.dot_general(a, b, (((1,), (1,)), ((), ())), preferred_element_type=F32)


def mm_tn(a, b):
    return lax.dot_general(a, b, (((0,), (0,)), ((), ())), preferred_element_type=F32)


def remote(src, dst, send, recv, device):
    return pltpu.make_async_remote_copy(
        src_ref=src,
        dst_ref=dst,
        send_sem=send,
        recv_sem=recv,
        device_id=device,
        device_id_type=MESH,
    )


def block(start, size, whole=128):
    return pl.ds(pl.multiple_of(start, whole), size)


class Place:
    def __init__(self):
        dp, cx, t = lax.axis_index("dp"), lax.axis_index("ctx"), lax.axis_index("tensor")
        self.dp, self.cx, self.t = dp, cx, t
        self.yy, self.core = lax.div(t, 2), lax.rem(t, 2)
        self.partner = (dp, 1 - cx, t)
        self.sibling = (dp, cx, t + 1 - 2 * self.core)
        self.across = (dp, cx, lax.rem(t + 2, 4))
        self.tensor_peers = [(dp, cx, lax.rem(t + k, 4)) for k in (1, 2, 3)]
        self.z_peers = [(lax.rem(dp + k, 4), cx, t) for k in (1, 2, 3)]
        self.spot = dp + cx * (7 - 2 * dp)
        self.right = self.at_spot(1)
        self.left = self.at_spot(-1)

    def at_spot(self, away):
        spot = lax.rem(self.spot + 8 + away, 8)
        cx = lax.div(spot, 4)
        return (spot + cx * (7 - 2 * spot), cx, self.t)

    def slab(self, away):
        dp, cx, _ = self.at_spot(away)
        return dp * 2 + cx

    def greet(self):
        barrier = pltpu.get_barrier_semaphore()
        peers = self.z_peers + [self.partner] + self.tensor_peers
        for peer in peers:
            pl.semaphore_signal(barrier, inc=1, device_id=peer, device_id_type=MESH)
        pl.semaphore_wait(barrier, len(peers))


class Ring:
    def __init__(self, place, send_sems, recv_sems):
        self.place, self.send_sems, self.recv_sems = place, send_sems, recv_sems

    def copy(self, d, e, s, src, dst):
        at = (d, e, s - 1)
        device = self.place.right if d == 0 else self.place.left
        return remote(src, dst, self.send_sems.at[at], self.recv_sems.at[at], device)


class TensorSum:
    def __init__(self, place, seg, cbuf, ysend, ybuf, kept, c_s, c_r, y_s, y_r, a_s, a_r):
        self.place, self.seg = place, seg
        self.slot = (0, 1, 1, 1)
        self.half, self.quarter = seg // 2, seg // 4
        self.cbuf, self.ysend, self.ybuf, self.kept = cbuf, ysend, ybuf, kept
        self.c_s, self.c_r, self.y_s, self.y_r, self.a_s, self.a_r = c_s, c_r, y_s, y_r, a_s, a_r

    def rows(self, m, c, y):
        return block(m * self.seg + c * self.half + y * self.quarter, self.quarter)

    def own_rows(self, m):
        return self.rows(m, self.place.core, self.place.yy)

    def c_copy(self, m, j, src):
        rows = block(m * self.seg + (1 - self.place.core) * self.half, self.half)
        return remote(
            src.at[rows], self.cbuf.at[m, self.slot[j]], self.c_s.at[m, j], self.c_r.at[m, j],
            self.place.sibling,
        )

    def y_copy(self, m, j):
        return remote(
            self.ysend.at[m, self.slot[j]], self.ybuf.at[m, self.slot[j]], self.y_s.at[m, j], self.y_r.at[m, j],
            self.place.across,
        )

    def to_quarters(self, m, j, src):
        self.c_copy(m, j, src).wait_recv()
        yy, core = self.place.yy, self.place.core
        near, far = block(yy * self.quarter, self.quarter), block((1 - yy) * self.quarter, self.quarter)
        other = src[self.rows(m, core, 1 - yy), :].astype(F32)
        self.ysend[m, self.slot[j]] = (other + self.cbuf[m, self.slot[j], far, :].astype(F32)).astype(BF)
        self.y_copy(m, j).start()
        mine = src[self.rows(m, core, yy), :].astype(F32)
        self.kept[m, self.slot[j]] = mine + self.cbuf[m, self.slot[j], near, :].astype(F32)

    def total(self, m, j):
        self.y_copy(m, j).wait_recv()
        return self.kept[m, self.slot[j]] + self.ybuf[m, self.slot[j]].astype(F32)

    def a_copy(self, m, j, ref, step, own=None):
        yy, core = self.place.yy, self.place.core
        spot = ref.at[self.rows(m, core, 1 - yy if step == 2 else yy)]
        source = spot if own is None or step == 2 else own
        return remote(
            source, spot, self.a_s.at[m, j, step], self.a_r.at[m, j, step],
            self.place.across if step == 0 else self.place.sibling,
        )

    def a_recv(self, m, j, ref, step):
        yy, core = self.place.yy, self.place.core
        spot = ref.at[
            self.rows(m, core if step == 0 else 1 - core, yy if step == 1 else 1 - yy)
        ]
        return remote(
            spot, spot, self.a_s.at[m, j, step], self.a_r.at[m, j, step], self.place.sibling
        )

    def share(self, m, j, ref, own=None):
        self.a_copy(m, j, ref, 0, own).start()
        self.a_copy(m, j, ref, 1, own).start()

    def pass_on(self, m, j, ref):
        self.a_recv(m, j, ref, 0).wait_recv()
        self.a_copy(m, j, ref, 2).start()

    def shared(self, m, j, ref):
        self.a_recv(m, j, ref, 1).wait_recv()
        self.a_recv(m, j, ref, 2).wait_recv()


def low_lanes(shape):
    return lax.rem(lax.broadcasted_iota(jnp.int32, shape, len(shape) - 1), 128) < 64


def head_lanes(h, base=0):
    return slice(base + h * 128, base + (h + 1) * 128)


def fill_bias(bias_ref, band_ref, heads):
    rows = lax.broadcasted_iota(jnp.int32, (BAND, 2 * BAND), 0)
    cols = lax.broadcasted_iota(jnp.int32, (BAND, 2 * BAND), 1)
    away = rows + BAND - cols

    def one_head(h, carry):
        tile = jnp.full((BAND, 2 * BAND), bias_ref[h, 0], F32)
        for b in range(1, BUCKETS):
            tile = jnp.where(away >= bucket_starts[b], bias_ref[h, b], tile)
        band_ref[h] = tile - bias_ref[h, BUCKETS - 1]
        return carry

    lax.fori_loop(0, heads, one_head, 0)


def masked_scores(q_tile, keys, band_ref, scores, h, first, length):
    count = keys.shape[0]
    scores[:, BAND:] = mm_nt(q_tile, keys) * 0.125
    for part in range(QT // BAND):
        spot = (block(part * BAND, BAND), block(first + part * BAND, 2 * BAND))
        scores[spot] = scores[spot] + band_ref[h]
    values = scores[:, BAND:]
    key_pos = lax.broadcasted_iota(jnp.int32, (QT, count), 1)
    query_pos = lax.broadcasted_iota(jnp.int32, (QT, count), 0) + first
    allowed = (key_pos <= query_pos) & (key_pos < length)
    return jnp.where(allowed, values, -1e30), allowed


def bucket_sums(heads, band_sum, whole_sum, dbias):
    rows = lax.broadcasted_iota(jnp.int32, (BAND, 2 * BAND), 0)
    cols = lax.broadcasted_iota(jnp.int32, (BAND, 2 * BAND), 1)
    away = rows + BAND - cols
    bucket = lax.broadcasted_iota(jnp.int32, (BUCKETS, 2 * BAND), 0)
    lanes128 = lax.broadcasted_iota(jnp.int32, (BUCKETS, 128), 1)

    def one_head(h, carry):
        tile = band_sum[h]
        sums = jnp.zeros((BUCKETS, 2 * BAND), F32)
        for b in range(BUCKETS - 1):
            inside = (away >= bucket_starts[b]) & (away < bucket_starts[b + 1])
            row = jnp.sum(jnp.where(inside, tile, 0.0), axis=0, keepdims=True)
            sums = jnp.where(bucket == b, row, sums)
        per_bucket = jnp.sum(sums, axis=1, keepdims=True)
        near = jnp.sum(per_bucket, axis=0, keepdims=True)
        total = jnp.sum(whole_sum[h, 0:1, :], axis=1, keepdims=True)
        last = lax.broadcasted_iota(jnp.int32, (BUCKETS, 1), 0) == BUCKETS - 1
        per_bucket = jnp.where(last, total - near, per_bucket)
        dbias[...] = jnp.where(lanes128 == h, per_bucket, dbias[...])
        return carry

    dbias[...] = jnp.zeros((BUCKETS, 128), F32)
    lax.fori_loop(0, heads, one_head, 0)


def norm_back(x, gain, grad):
    scale = lax.rsqrt(jnp.mean(x * x, axis=-1, keepdims=True) + 1e-06)
    unit = x * scale
    pulled = grad * gain
    inner = jnp.mean(pulled * unit, axis=-1, keepdims=True)
    return scale * (pulled - unit * inner), grad * unit


def layer_kernel(
    heads,
    len_ref,
    bias_ref,
    slot_lanes,
    tok,
    cot,
    wsmall,
    w,
    result,
    input_grad,
    w_grad,
    small_grad,
    tiny_out,
    dbias_out,
    w_full,
    ws_full,
    ws,
    gains,
    hidden,
    ntwo,
    q3,
    kv,
    lse,
    ab3,
    wbuf,
    gw,
    in_one,
    in_two,
    in_late,
    sx,
    sz,
    sum_grad,
    epart,
    npart,
    ffn,
    probs_ref,
    chosen_ref,
    cbuf,
    ysend,
    ybuf,
    kept,
    hgrad,
    bgrad,
    own_out,
    do3,
    grads,
    dkv_acc,
    dkv,
    band,
    scores,
    spread,
    band_sum,
    whole_sum,
    gg_own,
    gg_in,
    gg_sum,
    tiny_own,
    tiny_t,
    tiny_x,
    tiny_z,
    dbias_own,
    dbias_x,
    dbias_z,
    load_sem,
    out_sem,
    local,
    ready,
    gz_s,
    gz_r,
    gx_s,
    gx_r,
    k_s,
    k_r,
    ag_s,
    ag_r,
    rs_s,
    rs_r,
    c_s,
    c_r,
    y_s,
    y_r,
    a_s,
    a_r,
    kv_s,
    kv_r,
    gg_s,
    gg_r,
    sx_s,
    sx_r,
    sz_s,
    sz_r,
    tt_s,
    tt_r,
    tx_s,
    tx_r,
    tz_s,
    tz_r,
    bx_s,
    bx_r,
    bz_s,
    bz_r,
):
    place = Place()
    dp, cx, t = place.dp, place.cx, place.t
    seg = tok.shape[0] // 2
    width = tok.shape[1]
    shard = width // 8
    experts = w.shape[0]
    span = kv.shape[2]
    cap = slot_lanes.shape[2]
    place.greet()
    gather_ring = Ring(place, ag_s, ag_r)
    reduce_ring = Ring(place, rs_s, rs_r)
    sums = TensorSum(place, seg, cbuf, ysend, ybuf, kept, c_s, c_r, y_s, y_r, a_s, a_r)
    bpart = epart

    def small_slab(k, c):
        return lax.rem(dp + 4 - k, 4) * 2 + c

    def gz_copy(k, slab):
        return remote(
            wsmall, ws_full.at[slab], gz_s.at[k - 1], gz_r.at[k - 1], place.z_peers[k - 1]
        )

    def gx_copy(k, c):
        spot = ws_full.at[small_slab(k, c)]
        return remote(wsmall if k == 0 else spot, spot, gx_s.at[k], gx_r.at[k], place.partner)

    small_own = pltpu.make_async_copy(wsmall, ws_full.at[small_slab(0, cx)], local.at[experts])

    def gather(d, e, s, sending):
        away = s - 1 if sending else s
        slab = place.slab(-away if d == 0 else away)
        spot = w_full.at[e, d, slab] if s == 4 else w_full.at[e, :, slab]
        return gather_ring.copy(d, e, s, w.at[e] if sending and s == 1 else spot, spot)

    def w_own(e):
        return pltpu.make_async_copy(w.at[e], w_full.at[e, :, place.slab(0)], local.at[e])

    def gather_step(e, s):
        for d in range(2):
            if s > 1:
                gather(d, e, s - 1, False).wait_recv()
            gather(d, e, s, True).start()

    def landing(d, e, s):
        if s == 1:
            return in_one.at[d, e]
        if s == 2:
            return in_two.at[d, e]
        if e < 2:
            return in_late.at[s - 3, d, e]
        return wbuf.at[e, pl.ds(d * 4 + (s - 3) * 2, 2)]

    def reduce_copy(d, e, s):
        slab = place.slab(5 - s if d == 0 else s - 5)
        src = gw.at[e, d, slab] if s == 1 else gw.at[e, :, slab]
        return reduce_ring.copy(d, e, s, src, landing(d, e, s))

    def reduce_step(e, s):
        for d in range(2):
            if s > 1:
                slab = place.slab(5 - s if d == 0 else s - 5)
                reduce_copy(d, e, s - 1).wait_recv()
                came = landing(d, e, s - 1)

                def add(i, carry):
                    rows = block(i * 16, 16, 16)
                    if s == 2:
                        total = gw[e, d, slab, rows, :].astype(F32) + came[rows, :].astype(F32)
                        gw[e, d, slab, rows, :] = total.astype(BF)
                    else:
                        total = gw[e, :, slab, rows, :].astype(F32) + came[:, rows, :].astype(F32)
                        gw[e, :, slab, rows, :] = total.astype(BF)
                    return carry

                lax.fori_loop(0, shard // 16, add, 0)
            reduce_copy(d, e, s).start()

    def reduce_end(e):
        for d in range(2):
            reduce_copy(d, e, 4).wait_recv()

        def add(i, carry):
            rows = block(i * 16, 16, 16)
            total = gw[e, :, place.slab(0), rows, :].astype(F32)
            for d in range(2):
                total = total + landing(d, e, 4)[:, rows, :].astype(F32)
            w_grad[e, :, rows, :] = total
            return carry

        lax.fori_loop(0, shard // 16, add, 0)

    late = [(3, 2), (2, 3), (3, 3), (2, 4), (3, 4)]

    def pump_late(count=1):
        for _ in range(count):
            if late:
                reduce_step(*late.pop(0))

    small_own.start()
    for k in (1, 3, 2):
        gz_copy(k, small_slab(0, cx)).start()
    gx_copy(0, cx).start()
    for e in range(2):
        gather_step(e, 1)
    for e in range(experts):
        w_own(e).start()

    @pl.when(cx == 0)
    def _():
        for m in range(2):
            kv[m, seg:, :] = jnp.zeros((seg, span), BF)

    fill_bias(bias_ref, band, heads)
    spread[...] = jnp.zeros(spread.shape, F32)
    band_sum[...] = jnp.zeros(band_sum.shape, F32)
    whole_sum[...] = jnp.zeros(whole_sum.shape, F32)
    tiny_own[...] = jnp.zeros(tiny_own.shape, F32)
    for k in (1, 3, 2):
        gz_copy(k, small_slab(k, cx)).wait_recv()
        gx_copy(k, cx).start()
    small_own.wait()
    for k in range(4):
        gx_copy(k, 1 - cx).wait_recv()
    total = ws_full[0, shard:, :].astype(F32)
    for i in range(1, 8):
        total = total + ws_full[i, shard:, :].astype(F32)
    gains[...] = total
    for i in range(8):
        ws[i * shard : (i + 1) * shard, :] = ws_full[i, 0:shard, :]

    def first_norm(rows):
        x = tok[rows, :].astype(F32)
        scale = lax.rsqrt(jnp.mean(x * x, axis=-1, keepdims=True) + 1e-06)
        return (x * scale * gains[0:1, :]).astype(BF)

    def project(m):
        def step(i, carry):
            rows = block(m * seg + i * 256, 256)
            x = first_norm(rows)
            kv[m, block(cx * seg + i * 256, 256), :] = mm(x, ws[:, 0:span]).astype(BF)
            part = mm(x, ws[:, span:])
            q3[rows, :] = jnp.where(low_lanes(part.shape), part, 0.0).astype(BF)
            return carry

        lax.fori_loop(0, seg // 256, step, 0)

    def k_copy(m):
        spot = kv.at[m, block(0, seg), :]
        return remote(spot, spot, k_s.at[m], k_r.at[m], place.partner)

    for m in range(2):
        project(m)

        @pl.when(cx == 0)
        def _():
            k_copy(m).start()

        if m == 0:
            gather_step(0, 2)
        else:
            gather_step(1, 2)
            gather_step(2, 1)

    def attend(m):
        length = len_ref[m]

        def step(i, carry):
            rows = block(m * seg + i * QT, QT)
            first = cx * seg + i * QT
            lanes128 = lax.broadcasted_iota(jnp.int32, (QT, 128), 1)

            def one_head(h, tops):
                cut = block(h * 128, 128)
                values, allowed = masked_scores(
                    q3[rows, cut], kv[m, :, cut], band, scores, h, first, length
                )
                top = jnp.max(values, axis=-1, keepdims=True)
                raised = jnp.where(allowed, jnp.exp(values - top), 0.0)
                mass = jnp.sum(raised, axis=-1, keepdims=True)
                probs = (raised * (1.0 / mass)).astype(BF)
                part = mm(probs, kv[m, :, cut])
                ab3[rows, cut] = jnp.where(low_lanes(part.shape), 0.0, part).astype(BF)
                return jnp.where(lanes128 == h, top + jnp.log(mass), tops)

            lse[rows, :] = lax.fori_loop(0, heads, one_head, jnp.zeros((QT, 128), F32))
            bpart[rows, :] = mm_nt(ab3[rows, :], ws[:, span:]).astype(BF)
            return carry

        lax.fori_loop(0, seg // QT, step, 0)

    def second_norm(m):
        rows = sums.own_rows(m)
        x = tok[rows, :].astype(F32) + sums.total(m, 3)
        hidden[m] = x
        scale = lax.rsqrt(jnp.mean(x * x, axis=-1, keepdims=True) + 1e-06)
        ntwo[rows, :] = (x * scale * gains[1:2, :]).astype(BF)
        sums.share(m, 3, ntwo)

    for m in range(2):

        @pl.when(cx == 1)
        def _():
            k_copy(m).wait_recv()

        attend(m)
        sums.c_copy(m, 3, bpart).start()
        gather_step(m, 3)
        if m == 1:
            second_norm(0)
        sums.to_quarters(m, 3, bpart)
    gather_step(3, 1)
    second_norm(1)
    sums.pass_on(0, 3, ntwo)
    gather_step(0, 4)
    sums.pass_on(1, 3, ntwo)
    gather_step(1, 4)
    for m in range(2):
        sums.shared(m, 3, ntwo)
        sums.c_copy(m, 3, bpart).wait_send()

    router16 = gains[...].astype(BF)

    def upstream_of(rows, m, first):
        spot = lax.broadcasted_iota(jnp.int32, (rows.size, 1), 0) + (cx * seg + first)
        live = (spot < len_ref[m]).astype(F32)
        return live, live * cot[rows, :].astype(F32)

    def choices(m, carry):
        lanes = lax.broadcasted_iota(jnp.int32, (seg, 16), 1)
        chosen = jnp.zeros((seg, 16), F32)
        for e in range(experts):
            inside = put_of(m, e).astype(F32)
            chosen = jnp.where(lanes == e + 2, jnp.sum(inside, axis=1, keepdims=True), chosen)
        chosen_ref[block(m * seg, seg), :] = chosen
        return carry

    def put_of(m, e):
        row = slot_lanes[m, pl.ds(e, 1), :]
        return row == lax.broadcasted_iota(jnp.int32, (seg, cap), 0)

    lax.fori_loop(0, 2, choices, 0)

    def gates(i, carry):
        rows = block(i * 256, 256)
        m = lax.div(i, seg // 256)
        logits = mm_nt(ntwo[rows, :], router16)
        lanes = lax.broadcasted_iota(jnp.int32, (256, 16), 1)
        inside = (lanes >= 2) & (lanes < 2 + experts)
        logits = jnp.where(inside, logits, -1e30)
        top = jnp.max(logits, axis=-1, keepdims=True)
        raised = jnp.where(inside, jnp.exp(logits - top), 0.0)
        probs = raised / jnp.sum(raised, axis=-1, keepdims=True)
        probs_ref[rows, :] = probs
        gate = jnp.sum(probs * chosen_ref[rows, :], axis=-1, keepdims=True)
        live, upstream = upstream_of(rows, m, lax.rem(i, seg // 256) * 256)
        sum_grad[rows, :] = (gate * upstream).astype(BF)
        epart[rows, :] = jnp.zeros((256, width), BF)
        npart[rows, :] = jnp.zeros((256, width), BF)
        return carry

    lax.fori_loop(0, 2 * seg // 256, gates, 0)

    def load(e):
        slot = lax.rem(e, 2)
        return pltpu.make_async_copy(
            w_full.at[e], wbuf.at[pl.ds(slot * 2, 2)], load_sem.at[slot]
        )

    def arrived(e):
        w_own(e).wait()
        for d in range(2):
            gather(d, e, 4, False).wait_recv()
        load(e).start()

    picked, slot_grad, activated, raised_grad = (ffn.at[i] for i in range(4))

    def start_sums():
        for m in range(2):
            sums.c_copy(m, 1, npart).start()
            sums.c_copy(m, 0, epart).start()

    def g(e, s):
        return lambda: gather_step(e, s)

    def r(e, s):
        return lambda: reduce_step(e, s)

    def here(e):
        return lambda: arrived(e)

    before = ([here(0), here(1)], [], [], [])
    between = ([g(3, 2)], [g(3, 3)], [here(3)], [r(1, 4), start_sums])
    after = (
        [g(2, 3)],
        [g(2, 4), g(3, 4), r(0, 2), here(2), r(1, 2), r(0, 3)],
        [r(1, 3), r(0, 4)],
        [r(2, 2)],
    )

    def act_on(e, plan):
        for i, acts in enumerate(plan):
            if acts:

                @pl.when(e == i)
                def _(acts=acts):
                    for act in acts:
                        act()

    def expert(e, carry):
        slot = lax.rem(e, 2)

        def weight(which):
            return wbuf[slot * 2 + which].reshape(width, -1)

        act_on(e, before)
        load(e).wait()

        def one_micro(m, carry):
            rows = block(m * seg, seg)
            slots = block(m * cap, cap)
            put = put_of(m, e).astype(BF)
            chosen_rows = mm_tn(put, ntwo[rows, :]).astype(BF)
            picked[slots, :] = chosen_rows
            slot_part = mm_tn(put, sum_grad[rows, :]).astype(BF)
            slot_grad[slots, :] = slot_part
            raised = mm(chosen_rows, weight(0))
            square = raised * raised
            bent = jnp.tanh(C0 * raised * (1.0 + C1 * square))
            cdf = 0.5 * (1.0 + bent)
            act = (raised * cdf).astype(BF)
            activated[slots, :] = act
            slope = cdf + 0.5 * raised * (1.0 - bent * bent) * (C0 * (1.0 + 3.0 * C1 * square))
            act_grad = mm(slot_part, weight(1))
            back = (act_grad * slope).astype(BF)
            raised_grad[slots, :] = back
            lowered = mm_nt(act, weight(1)).astype(BF)
            epart[rows, :] += mm(put, lowered).astype(BF)
            pulled = mm_nt(back, weight(0)).astype(BF)
            npart[rows, :] += mm(put, pulled).astype(BF)
            return carry

        lax.fori_loop(0, 2, one_micro, 0)
        act_on(e, between)

        def weight_part(i, carry):
            lanes = block(i * 384, 384)
            slabs = pl.ds(i * 4, 4)
            part = mm_tn(picked[:, lanes], raised_grad[...]).astype(BF)
            gw[e, 0, slabs] = part.reshape(4, shard, -1)
            part = mm_tn(slot_grad[:, lanes], activated[...]).astype(BF)
            gw[e, 1, slabs] = part.reshape(4, shard, -1)
            return carry

        lax.fori_loop(0, width // 384, weight_part, 0)
        reduce_step(e, 1)
        act_on(e, after)
        return carry

    gather_step(2, 2)
    lax.fori_loop(0, experts, expert, 0)

    for peer in (place.right, place.left):
        pl.semaphore_signal(ready, inc=1, device_id=peer, device_id_type=MESH)

    ones = jnp.ones((8, width), BF)
    for m in range(2):

        def gate_terms(i, carry):
            rows = block(m * seg + i * 256, 256)
            live, upstream = upstream_of(rows, m, i * 256)
            terms = epart[rows, :].astype(F32) * upstream
            high = terms.astype(BF)
            rest = (terms - high.astype(F32)).astype(BF)
            gg_own[m, :, block(i * 256, 256)] = mm_nt(ones, high) + mm_nt(ones, rest)
            return carry

        sums.y_copy(m, 3).wait_send()
        sums.to_quarters(m, 1, npart)
        lax.fori_loop(0, seg // 256, gate_terms, 0)

    def gg_copy(k):
        return remote(gg_own, gg_in.at[k - 1], gg_s.at[k - 1], gg_r.at[k - 1], place.tensor_peers[k - 1])

    for k in (1, 2, 3):
        gg_copy(k).start()
    pump_late()
    pl.semaphore_wait(ready, 2)
    for k in (1, 2, 3):
        gg_copy(k).wait_recv()
    gg_sum[...] = gg_own[...] + gg_in[0] + gg_in[1] + gg_in[2]
    own_first = place.core * (seg // 2) + place.yy * (seg // 4)

    def own_copy(m, j, ref):
        return pltpu.make_async_copy(
            own_out.at[m, j - 1], ref.at[sums.own_rows(m)], out_sem.at[m * 2 + j - 1]
        )

    for m in range(2):
        rows = sums.own_rows(m)
        line = gg_sum[m, :, block(own_first, seg // 4)]
        line = jnp.where(lax.broadcasted_iota(jnp.int32, line.shape, 0) == 0, line, 0.0)
        high = line.astype(BF)
        rest = (line - high.astype(F32)).astype(BF)
        ones = jnp.ones((8, 128), BF)
        gate_grad = (mm_tn(high, ones) + mm_tn(rest, ones))[:, 0:1]
        down = sums.total(m, 1)
        live, upstream = upstream_of(rows, m, own_first)
        probs, chosen = probs_ref[rows, :], chosen_ref[rows, :]
        gate = jnp.sum(probs * chosen, axis=-1, keepdims=True)
        logit_grad = (probs * gate_grad * (chosen - gate)).astype(BF)
        down = down + mm(logit_grad, router16)
        through, gain_terms = norm_back(hidden[m], gains[1:2, :], down)
        full = through + upstream
        hgrad[m] = full
        bgrad[rows, :] = full.astype(BF)
        sums.share(m, 0, bgrad)
        tiny_own[1:2, :] += jnp.sum(gain_terms, axis=0, keepdims=True)
        tiny_own[...] += mm_tn(logit_grad, ntwo[rows, :])[0:8, :]
    pump_late()
    for m in range(2):
        sums.pass_on(m, 0, bgrad)
    for m in range(2):
        sums.to_quarters(m, 0, epart)

    def dkv_copy(m, h):
        spot = dkv.at[m, h]
        return remote(spot, spot, kv_s.at[m, h], kv_r.at[m, h], place.partner)

    def attend_back(m):
        length = len_ref[m]

        def lower(i, carry):
            part = mm(bgrad[block(m * seg + i * 256, 256), :], ws[:, span:])
            part = jnp.where(low_lanes(part.shape), 0.0, part)
            do3[block(i * 256, 256), :] = part.astype(BF)
            return carry

        lax.fori_loop(0, seg // 256, lower, 0)

        def one_head(h, carry):
            cut = block(h * 128, 128)
            dkv_acc[...] = jnp.zeros(dkv_acc.shape, F32)

            def step(i, carry):
                rows = block(m * seg + i * QT, QT)
                first = cx * seg + i * QT
                q_tile, do_tile = q3[rows, cut], do3[block(i * QT, QT), cut]
                keys = kv[m, :, cut]
                values, allowed = masked_scores(q_tile, keys, band, scores, h, first, length)
                lanes128 = lax.broadcasted_iota(jnp.int32, (QT, 128), 1)
                mass = jnp.sum(jnp.where(lanes128 == h, lse[rows, :], 0.0), axis=1, keepdims=True)
                soft = jnp.where(allowed, jnp.exp(values - mass), 0.0)
                soft_grad = mm_nt(do_tile, keys)
                delta = jnp.sum(soft * soft_grad, axis=-1, keepdims=True)
                score_grad = (soft * (soft_grad - delta)).astype(BF)
                dkv_acc[...] += mm_tn(soft.astype(BF), do_tile) + 0.125 * mm_tn(score_grad, q_tile)
                part = mm(score_grad, keys) * 0.125
                grads[rows, block(span + h * 128, 128)] = jnp.where(
                    low_lanes(part.shape), part, 0.0
                ).astype(BF)
                spread[:, BAND:] = score_grad.astype(F32)
                for half in range(QT // BAND):
                    lanes = block(first + half * BAND, 2 * BAND)
                    band_sum[h] += spread[half * BAND : (half + 1) * BAND, lanes]
                whole_sum[h, 0:1, :] += jnp.sum(spread[:, BAND:], axis=0, keepdims=True)
                return carry

            lax.fori_loop(0, seg // QT, step, 0)

            @pl.when(cx == 1)
            def _():
                dkv[m, h] = dkv_acc[0:seg, :].astype(BF)
                dkv_copy(m, h).start()

            grads[pl.ds(m * seg, seg), cut] = dkv_acc[block(cx * seg, seg), :].astype(BF)

            @pl.when(h == 1)
            def _():
                pump_late()

            return carry

        lax.fori_loop(0, heads, one_head, 0)

    def after_attend(m):
        rows = pl.ds(m * seg, seg)

        @pl.when(cx == 0)
        def _():
            for h in range(heads):
                dkv_copy(m, h).wait_recv()
                total = grads[rows, head_lanes(h)].astype(F32) + dkv[m, h].astype(F32)
                grads[rows, head_lanes(h)] = total.astype(BF)

        def lower(i, carry):
            spot = block(m * seg + i * 256, 256)
            npart[spot, :] = mm_nt(grads[spot, :], ws[...]).astype(BF)
            return carry

        lax.fori_loop(0, seg // 256, lower, 0)
        sums.c_copy(m, 2, npart).start()

    def gs_spot(slab, half):
        return ws_full.at[slab, pl.ds(0, shard), pl.ds(half * span, span)]

    def sx_copy(half, k):
        slab = lax.rem(dp + k, 4) * 2 + 1 - cx
        return remote(
            gs_spot(slab, half), sx.at[half, k], sx_s.at[half, k], sx_r.at[half, k], place.partner
        )

    def sz_copy(half, k):
        return remote(
            sx.at[half, k], sz.at[half, k - 1], sz_s.at[half, k - 1], sz_r.at[half, k - 1],
            place.z_peers[k - 1],
        )

    order = (2, 1, 3, 0)

    def small_part(half):
        def step(i, carry):
            lanes = block(i * 384, 384)
            cols = slice(half * span, (half + 1) * span)
            part = mm_tn(ffn[0, :, lanes], grads[0:seg, cols])
            part = part + mm_tn(ffn[1, :, lanes], grads[seg:, cols])
            if half == 1:
                part = part + mm_tn(bgrad[:, lanes], ab3[...])
            ws_full[pl.ds(i * 4, 4), 0:shard, cols] = part.astype(BF).reshape(4, shard, -1)
            return carry

        lax.fori_loop(0, width // 384, step, 0)
        for k in order:
            sx_copy(half, k).start()

    def small_step(half):
        cols = slice(half * span, (half + 1) * span)
        for k in order:
            sx_copy(half, k).wait_recv()
            slab = lax.rem(dp + k, 4) * 2 + cx
            total = ws_full[slab, 0:shard, cols].astype(F32) + sx[half, k].astype(F32)
            if k == 0:
                small_grad[:, cols] = total
            else:
                sx[half, k] = total.astype(BF)
                sz_copy(half, k).start()

    for m in range(2):
        sums.shared(m, 0, bgrad)
        attend_back(m)
        if m == 0:
            for i in range(2):

                def own_result(i):
                    rows = sums.own_rows(i)
                    expert_sum = sums.total(i, 0)
                    spot = lax.broadcasted_iota(jnp.int32, (seg // 4, 1), 0) + (cx * seg + own_first)
                    live = (spot < len_ref[i]).astype(F32)
                    gate = jnp.sum(probs_ref[rows, :] * chosen_ref[rows, :], axis=-1, keepdims=True)
                    own_out[i, 0] = (live * (hidden[i] + gate * expert_sum)).astype(BF)
                    own_copy(i, 1, result).start()
                    sums.share(i, 1, result, own_out.at[i, 0])

                own_result(i)

    def normed_again(i, carry):
        ffn[lax.div(i, 2), block(lax.rem(i, 2) * 256, 256), :] = first_norm(block(i * 256, 256))
        return carry

    lax.fori_loop(0, 2 * seg // 256, normed_again, 0)
    for k in range(4):
        gx_copy(k, cx).wait_send()
    small_part(1)
    sums.c_copy(0, 1, npart).wait_send()
    sums.y_copy(0, 1).wait_send()
    after_attend(0)
    sums.c_copy(1, 1, npart).wait_send()
    sums.y_copy(1, 1).wait_send()
    sums.to_quarters(0, 2, npart)
    after_attend(1)
    small_part(0)
    sums.to_quarters(1, 2, npart)
    pump_late(len(late))

    for m in range(2):
        down = sums.total(m, 2)
        rows = sums.own_rows(m)
        through, gain_terms = norm_back(tok[rows, :].astype(F32), gains[0:1, :], down)
        own_out[m, 1] = (through + hgrad[m]).astype(BF)
        sums.share(m, 2, input_grad, own_out.at[m, 1])
        own_copy(m, 2, input_grad).start()
        tiny_own[0:1, :] += jnp.sum(gain_terms, axis=0, keepdims=True)

    def tt_copy(k):
        return remote(
            tiny_own, tiny_t.at[k - 1], tt_s.at[k - 1], tt_r.at[k - 1], place.tensor_peers[k - 1]
        )

    for k in (1, 2, 3):
        tt_copy(k).start()
    small_step(1)
    small_step(0)
    for k in (1, 2, 3):
        tt_copy(k).wait_recv()
    tiny_x[0] = tiny_own[...] + tiny_t[0] + tiny_t[1] + tiny_t[2]
    tx_copy = remote(tiny_x.at[0], tiny_x.at[1], tx_s.at[0], tx_r.at[0], place.partner)
    tx_copy.start()
    bucket_sums(heads, band_sum, whole_sum, dbias_own)
    bx_copy = remote(dbias_own, dbias_x, bx_s.at[0], bx_r.at[0], place.partner)
    bx_copy.start()
    for m in range(2):
        sums.pass_on(m, 1, result)
        sums.pass_on(m, 2, input_grad)
    tx_copy.wait_recv()
    tiny_x[2] = tiny_x[0] + tiny_x[1]
    bx_copy.wait_recv()
    dbias_sum = dbias_own[...] + dbias_x[...]
    dbias_out[...] = dbias_sum

    def tz_copy(k):
        return remote(
            tiny_x.at[2], tiny_z.at[k - 1], tz_s.at[k - 1], tz_r.at[k - 1], place.z_peers[k - 1]
        )

    def bz_copy(k):
        return remote(
            dbias_out, dbias_z.at[k - 1], bz_s.at[k - 1], bz_r.at[k - 1], place.z_peers[k - 1]
        )

    for k in (1, 2, 3):
        tz_copy(k).start()
        bz_copy(k).start()
    for e in range(experts):
        reduce_end(e)
    for half in range(2):
        cols = slice(half * span, (half + 1) * span)
        total = small_grad[:, cols]
        for k in (1, 2, 3):
            sz_copy(half, k).wait_recv()
            total = total + sz[half, k - 1].astype(F32)
        small_grad[:, cols] = total
    for k in (1, 2, 3):
        bz_copy(k).wait_recv()
        bz_copy(k).wait_send()
        dbias_sum = dbias_sum + dbias_z[k - 1]
    dbias_out[...] = dbias_sum
    total = tiny_x[2]
    for k in (1, 2, 3):
        tz_copy(k).wait_recv()
        total = total + tiny_z[k - 1]
    tiny_out[...] = total
    for m in range(2):
        sums.shared(m, 1, result)
        sums.shared(m, 2, input_grad)

    for e in range(experts):
        for d in range(2):
            for s in (1, 2, 3, 4):
                gather(d, e, s, True).wait_send()
                reduce_copy(d, e, s).wait_send()
    for k in range(4):
        for half in range(2):
            sx_copy(half, k).wait_send()
            if k > 0:
                sz_copy(half, k).wait_send()
        if k > 0:
            gz_copy(k, small_slab(0, cx)).wait_send()
            gg_copy(k).wait_send()
            tt_copy(k).wait_send()
            tz_copy(k).wait_send()
    tx_copy.wait_send()
    bx_copy.wait_send()
    for m in range(2):
        sums.c_copy(m, 0, epart).wait_send()
        sums.c_copy(m, 2, npart).wait_send()
        own_copy(m, 1, result).wait()
        own_copy(m, 2, input_grad).wait()
        sums.y_copy(m, 0).wait_send()
        sums.y_copy(m, 2).wait_send()
        for j in range(4):
            for step in range(3):
                own = own_out.at[m, j - 1] if j in (1, 2) else None
                ref = (bgrad, result, input_grad, ntwo)[j]
                sums.a_copy(m, j, ref, step, own).wait_send()

        @pl.when(cx == 0)
        def _():
            k_copy(m).wait_send()

        @pl.when(cx == 1)
        def _():
            for h in range(heads):
                dkv_copy(m, h).wait_send()


def layer_call(lengths, bias, slot_lanes, tok, cot, wsmall, w):
    heads = bias.shape[0]
    rows, width = tok.shape
    span = heads * 128
    experts, ff = w.shape[0], w.shape[3]
    seg = rows // 2
    quarter = seg // 4
    shard = width // 8
    slots = 2 * slot_lanes.shape[2]
    vm = pl.BlockSpec(memory_space=pltpu.VMEM)
    sm = pl.BlockSpec(memory_space=pltpu.SMEM)
    hbm = pl.BlockSpec(memory_space=pl.ANY)
    dma = pltpu.SemaphoreType.DMA
    sds = jax.ShapeDtypeStruct
    low, full = (lambda *shape: pltpu.VMEM(shape, BF)), (lambda *shape: pltpu.VMEM(shape, F32))

    def pair(*shape):
        return [dma(shape), dma(shape)]

    return pl.pallas_call(
        functools.partial(layer_kernel, heads),
        out_shape=(
            sds((rows, width), BF),
            sds((rows, width), BF),
            sds((experts, 2, shard, ff), F32),
            sds((shard, width), F32),
            sds((8, width), F32),
            sds((BUCKETS, 128), F32),
            sds((experts, 2, 8, shard, ff), BF),
        ),
        in_specs=[sm, sm] + [vm] * 3 + [hbm] * 2,
        out_specs=(hbm,) * 2 + (vm,) * 4 + (hbm,),
        scratch_shapes=[
            low(8, *wsmall.shape),
            low(width, width),
            full(16, width),
            full(2, quarter, width),
            low(rows, width),
            low(rows, span),
            low(2, rows, span),
            full(rows, 128),
            low(rows, span),
            low(4, 8, shard, ff),
            low(experts, 2, 8, shard, ff),
            low(2, experts, shard, ff),
            low(2, experts, 2, shard, ff),
            low(2, 2, 2, 2, shard, ff),
            low(2, 4, shard, span),
            low(2, 3, shard, span),
            low(rows, width),
            low(rows, width),
            low(rows, width),
            low(4, slots, width),
            full(rows, 16),
            full(rows, 16),
            low(2, 2, 2 * quarter, width),
            low(2, 2, quarter, width),
            low(2, 2, quarter, width),
            full(2, 2, quarter, width),
            full(2, quarter, width),
            low(rows, width),
            low(2, 2, quarter, width),
            low(seg, span),
            low(rows, 2 * span),
            full(rows, 128),
            low(2, heads, seg, 128),
            full(heads, BAND, 2 * BAND),
            full(QT, rows + BAND),
            full(QT, rows + BAND),
            full(heads, BAND, 2 * BAND),
            full(heads, 8, rows),
            full(2, 8, seg),
            full(3, 2, 8, seg),
            full(2, 8, seg),
            full(8, width),
            full(3, 8, width),
            full(3, 8, width),
            full(3, 8, width),
            full(BUCKETS, 128),
            full(BUCKETS, 128),
            full(3, BUCKETS, 128),
            dma((2,)),
            dma((4,)),
            dma((experts + 1,)),
            pltpu.SemaphoreType.REGULAR,
        ]
        + pair(3)
        + pair(4)
        + pair(2)
        + pair(2, experts, 4)
        + pair(2, experts, 4)
        + pair(2, 4)
        + pair(2, 4)
        + pair(2, 4, 3)
        + pair(2, heads)
        + pair(3)
        + pair(2, 4)
        + pair(2, 3)
        + pair(3)
        + pair(1)
        + pair(3)
        + pair(1)
        + pair(3),
        compiler_params=pltpu.CompilerParams(
            collective_id=0, has_side_effects=True, vmem_limit_bytes=63 << 20
        ),
    )(lengths, bias, slot_lanes, tok, cot, wsmall, w)


def body_fast(
    inputs, lengths, expert_ids, slot_rows, attn_gain, qkv_weight, out_weight, position_bias,
    ffn_gain, router_weight, up_weight, down_weight, cotangent,
):
    micro, seg, width = inputs.shape
    rows = micro * seg
    experts = up_weight.shape[0]
    heads = position_bias.shape[1]
    size = qkv_weight.shape[2] // heads
    slab = lax.axis_index("dp") * 2 + lax.axis_index("ctx")
    shard = attn_gain.shape[0]
    by_head = jnp.concatenate(
        [
            qkv_weight[1].reshape(shard, heads, 1, size),
            qkv_weight[2].reshape(shard, heads, 1, size),
        ],
        axis=2,
    ).reshape(shard, -1)
    by_query = jnp.concatenate(
        [
            qkv_weight[0].reshape(shard, heads, 1, size),
            out_weight.T.reshape(shard, heads, 1, size),
        ],
        axis=2,
    ).reshape(shard, -1)
    small = jnp.concatenate(
        [attn_gain[None], ffn_gain[None], router_weight.T, jnp.zeros((10, shard), BF)], axis=0
    )
    small = lax.dynamic_update_slice(jnp.zeros((16, width), BF), small, (0, slab * shard))
    wsmall = jnp.concatenate([jnp.concatenate([by_head, by_query], axis=1), small], axis=0)
    w = jnp.stack([up_weight, jnp.transpose(down_weight, (0, 2, 1))], axis=1)
    tok = inputs.reshape(rows, width)
    result, input_part, w_grad, small_grad, tiny, dbias, _ = layer_call(
        lengths, position_bias.T, slot_rows.reshape(micro, experts, -1), tok,
        cotangent.reshape(rows, width), wsmall, w,
    )
    tiny = lax.dynamic_slice_in_dim(tiny, slab * shard, shard, axis=1)
    parts = small_grad.reshape(shard, 2, heads, 2, size)
    qkv_grad = jnp.stack(
        [parts[:, 1, :, 0], parts[:, 0, :, 0], parts[:, 0, :, 1]], axis=0
    ).reshape(3, shard, heads * size)
    return (
        result.reshape(inputs.shape),
        input_part.reshape(inputs.shape),
        tiny[0],
        qkv_grad,
        parts[:, 1, :, 1].reshape(shard, heads * size).T,
        dbias[:, :heads],
        tiny[1],
        tiny[2 : 2 + experts].T,
        w_grad[:, 0],
        jnp.transpose(w_grad[:, 1], (0, 2, 1)),
    )


def rms_norm(values, gain_vector):
    return (
        values * lax.rsqrt(jnp.mean(values * values, axis=-1, keepdims=True) + 1e-06) * gain_vector
    )


def bucket_of(distance):
    clipped = jnp.maximum(distance, 0)
    edge_values = jnp.asarray(bucket_edges, dtype=jnp.int32)
    beyond = jnp.sum((clipped[..., None] >= edge_values).astype(jnp.int32), axis=-1)
    return jnp.where(clipped < 16, clipped, jnp.minimum(16 + beyond, 31))


def toeplitz(diagonal, query_count, key_count):
    head_count = diagonal.shape[0]
    padded = jnp.pad(diagonal, ((0, 0), (0, 1)))
    row_width = query_count + key_count
    repeated = jnp.broadcast_to(padded[:, None, :], (head_count, query_count, row_width)).reshape(
        head_count, query_count * row_width
    )
    repeated = jnp.pad(repeated, ((0, 0), (0, query_count))).reshape(
        head_count, query_count, row_width + 1
    )[:, :, :key_count]
    return repeated[:, :, ::-1]


def diagonal_sums(gradient):
    head_count, query_count, key_count = gradient.shape
    offset_count = query_count + key_count - 1
    flipped = jnp.pad(gradient[:, :, ::-1], ((0, 0), (0, 0), (0, query_count)))
    skewed = flipped.reshape(head_count, query_count * (offset_count + 1))[
        :, : query_count * offset_count
    ]
    return jnp.sum(skewed.reshape(head_count, query_count, offset_count), axis=1)


def bucket_table(query_first, query_count, key_count):
    offsets = (
        query_first - (key_count - 1) + jnp.arange(query_count + key_count - 1, dtype=jnp.int32)
    )
    return (bucket_of(offsets)[:, None] == jnp.arange(BUCKETS, dtype=jnp.int32)[None, :]).astype(
        jnp.float32
    )


def body(
    inputs,
    lengths,
    expert_ids,
    slot_rows,
    attn_gain,
    qkv_weight,
    out_weight,
    position_bias,
    ffn_gain,
    router_weight,
    up_weight,
    down_weight,
    cotangent,
):
    highest = lax.Precision.HIGHEST
    micro_count, seg_rows, model_width = inputs.shape
    local_heads = position_bias.shape[1]
    head_size = qkv_weight.shape[2] // local_heads
    expert_count = up_weight.shape[0]
    query_first = lax.axis_index("ctx") * seg_rows
    query_pos = query_first + jnp.arange(seg_rows, dtype=jnp.int32)

    def pair_scores(query_heads, query_start, key_heads, length):
        query_count = query_heads.shape[0]
        key_count = key_heads.shape[0]
        scores = (
            jnp.einsum("qhd,khd->hqk", query_heads, key_heads, preferred_element_type=jnp.float32)
            * 0.125
        )
        diagonal = jnp.einsum(
            "rb,bh->hr",
            bucket_table(query_start, query_count, key_count),
            position_bias,
            precision=highest,
        )
        scores = scores + toeplitz(diagonal, query_count, key_count)
        query_place = query_start + jnp.arange(query_count, dtype=jnp.int32)
        key_place = jnp.arange(key_count, dtype=jnp.int32)
        allowed = (key_place[None, :] <= query_place[:, None]) & (key_place[None, :] < length)
        return (scores, allowed)

    def scores_for(query_heads, key_block, length):
        key_count = key_block.shape[0]
        key_heads = key_block.reshape(key_count, local_heads, head_size)
        scores, allowed = pair_scores(query_heads, query_first, key_heads, length)
        return (scores, allowed, key_heads)

    results = []
    input_parts = []
    grad_sums = None
    bias_total = jnp.zeros((local_heads, BUCKETS), jnp.float32)
    for micro_step in range(micro_count):
        forward_gain_one = lax.all_gather(attn_gain, ("dp", "ctx"), axis=0, tiled=True)
        forward_qkv_full = lax.all_gather(qkv_weight, ("dp", "ctx"), axis=1, tiled=True)
        forward_out_full = lax.all_gather(out_weight, ("dp", "ctx"), axis=1, tiled=True)
        forward_gain_two = lax.all_gather(ffn_gain, ("dp", "ctx"), axis=0, tiled=True)
        forward_router_full = lax.all_gather(router_weight, ("dp", "ctx"), axis=0, tiled=True)
        forward_up_full = lax.all_gather(up_weight, ("dp", "ctx"), axis=1, tiled=True)
        forward_down_full = lax.all_gather(down_weight, ("dp", "ctx"), axis=2, tiled=True)
        forward_tokens = inputs[micro_step].astype(jnp.float32)
        forward_length = lengths[micro_step]
        forward_normed = rms_norm(forward_tokens, forward_gain_one.astype(jnp.float32)).astype(
            jnp.bfloat16
        )
        forward_projected = jnp.einsum(
            "td,cde->cte", forward_normed, forward_qkv_full, preferred_element_type=jnp.float32
        ).astype(jnp.bfloat16)
        forward_query_heads = forward_projected[0].reshape(seg_rows, local_heads, head_size)
        row_top = jnp.full((local_heads, seg_rows), -1e30, jnp.float32)
        attend_scores, attend_allowed, attend_key_heads = scores_for(
            forward_query_heads,
            lax.all_gather(forward_projected[1], "ctx", axis=0, tiled=True),
            forward_length,
        )
        value_heads = lax.all_gather(forward_projected[2], "ctx", axis=0, tiled=True).reshape(
            attend_key_heads.shape
        )
        attend_scores = jnp.where(attend_allowed[None], attend_scores, -1e30)
        new_top = jnp.maximum(row_top, jnp.max(attend_scores, axis=-1))
        weights_exp = jnp.where(
            attend_allowed[None], jnp.exp(attend_scores - new_top[:, :, None]), 0.0
        )
        row_total = jnp.sum(weights_exp, axis=-1)
        summed = jnp.einsum(
            "hqk,khd->hqd",
            weights_exp.astype(jnp.bfloat16),
            value_heads,
            preferred_element_type=jnp.float32,
        )
        row_top, row_total, summed = (new_top, row_total, summed)
        forward_attended = summed / row_total[:, :, None]
        forward_log_total = row_top + jnp.log(row_total)
        forward_attended_low = (
            jnp.transpose(forward_attended, (1, 0, 2)).reshape(seg_rows, -1).astype(jnp.bfloat16)
        )
        branch = lax.psum(
            jnp.dot(
                forward_attended_low, forward_out_full, preferred_element_type=jnp.float32
            ).astype(jnp.bfloat16),
            "tensor",
        ).astype(jnp.float32)
        forward_hidden = forward_tokens + branch
        forward_normed_two = rms_norm(forward_hidden, forward_gain_two.astype(jnp.float32)).astype(
            jnp.bfloat16
        )
        logits = jnp.dot(
            forward_normed_two, forward_router_full, preferred_element_type=jnp.float32
        )
        forward_router_probs = jax.nn.softmax(logits, axis=-1)
        forward_chosen = (
            expert_ids[micro_step][:, None] == jnp.arange(expert_count, dtype=jnp.int32)[None, :]
        ).astype(jnp.float32)
        forward_gate_value = jnp.sum(forward_router_probs * forward_chosen, axis=-1)
        forward_slot_table = slot_rows[micro_step, 0]
        padded = jnp.concatenate(
            [forward_normed_two, jnp.zeros((1, model_width), jnp.bfloat16)], axis=0
        )
        forward_picked = padded[forward_slot_table]
        forward_raised = jnp.einsum(
            "ekd,edf->ekf", forward_picked, forward_up_full, preferred_element_type=jnp.float32
        )
        forward_activated = jax.nn.gelu(forward_raised).astype(jnp.bfloat16)
        lowered = jnp.einsum(
            "ekf,efd->ekd", forward_activated, forward_down_full, preferred_element_type=jnp.float32
        )
        spread = (
            jnp.zeros((seg_rows + 1, model_width), jnp.float32)
            .at[forward_slot_table.reshape(-1)]
            .add(lowered.reshape(-1, model_width))[:seg_rows]
        )
        forward_expert_sum = lax.psum(spread.astype(jnp.bfloat16), "tensor").astype(jnp.float32)
        forward_live_rows = (query_pos < forward_length).astype(jnp.float32)[:, None]
        result = (
            forward_live_rows * (forward_hidden + forward_gate_value[:, None] * forward_expert_sum)
        ).astype(jnp.bfloat16)
        forward_kept_state = (
            forward_tokens,
            forward_length,
            forward_normed,
            forward_projected,
            forward_attended,
            forward_log_total,
            forward_attended_low,
            forward_hidden,
            forward_normed_two,
            forward_router_probs,
            forward_chosen,
            forward_gate_value,
            forward_slot_table,
            forward_picked,
            forward_raised,
            forward_activated,
            forward_expert_sum,
            forward_live_rows,
        )
        result, kept_state = (result, forward_kept_state)
        gain_one = lax.all_gather(attn_gain, ("dp", "ctx"), axis=0, tiled=True)
        qkv_full = lax.all_gather(qkv_weight, ("dp", "ctx"), axis=1, tiled=True)
        out_full = lax.all_gather(out_weight, ("dp", "ctx"), axis=1, tiled=True)
        gain_two = lax.all_gather(ffn_gain, ("dp", "ctx"), axis=0, tiled=True)
        router_full = lax.all_gather(router_weight, ("dp", "ctx"), axis=0, tiled=True)
        up_full = lax.all_gather(up_weight, ("dp", "ctx"), axis=1, tiled=True)
        down_full = lax.all_gather(down_weight, ("dp", "ctx"), axis=2, tiled=True)
        (
            tokens,
            backward_length,
            normed,
            projected,
            attended,
            log_total,
            attended_low,
            hidden,
            normed_two,
            router_probs,
            chosen,
            gate_value,
            slot_table,
            picked,
            raised,
            activated,
            expert_sum,
            live_rows,
        ) = kept_state
        upstream = live_rows * cotangent[micro_step].astype(jnp.float32)
        sum_grad = (gate_value[:, None] * upstream).astype(jnp.bfloat16)
        gate_grad = jnp.sum(expert_sum * upstream, axis=-1)
        logit_grad = (router_probs * gate_grad[:, None] * (chosen - gate_value[:, None])).astype(
            jnp.bfloat16
        )
        router_part = jnp.einsum(
            "td,te->de", normed_two, logit_grad, preferred_element_type=jnp.float32
        )
        padded_grad = jnp.concatenate([sum_grad, jnp.zeros((1, model_width), jnp.bfloat16)], axis=0)
        slot_grad = padded_grad[slot_table]
        down_part = jnp.einsum(
            "ekf,ekd->efd", activated, slot_grad, preferred_element_type=jnp.float32
        )
        act_grad = jnp.einsum(
            "ekd,efd->ekf", slot_grad, down_full, preferred_element_type=jnp.float32
        )
        unused_value, gelu_back = jax.vjp(jax.nn.gelu, raised)
        raised_grad = gelu_back(act_grad)[0].astype(jnp.bfloat16)
        up_part = jnp.einsum(
            "ekd,ekf->edf", picked, raised_grad, preferred_element_type=jnp.float32
        )
        picked_grad = jnp.einsum(
            "ekf,edf->ekd", raised_grad, up_full, preferred_element_type=jnp.float32
        )
        spread_grad = (
            jnp.zeros((seg_rows + 1, model_width), jnp.float32)
            .at[slot_table.reshape(-1)]
            .add(picked_grad.reshape(-1, model_width))[:seg_rows]
        )
        normed_two_grad = lax.psum(spread_grad.astype(jnp.bfloat16), "tensor").astype(
            jnp.float32
        ) + jnp.einsum("te,de->td", logit_grad, router_full, preferred_element_type=jnp.float32)
        unused_norm, second_back = jax.vjp(rms_norm, hidden, gain_two.astype(jnp.float32))
        hidden_grad, gain_two_part = second_back(normed_two_grad)
        hidden_grad = hidden_grad + upstream
        branch_grad = hidden_grad.astype(jnp.bfloat16)
        out_part = jnp.einsum(
            "te,td->ed", attended_low, branch_grad, preferred_element_type=jnp.float32
        )
        attended_grad = jnp.einsum(
            "td,ed->te", branch_grad, out_full, preferred_element_type=jnp.float32
        ).astype(jnp.bfloat16)
        grad_heads = attended_grad.reshape(seg_rows, local_heads, head_size)
        row_delta = jnp.sum(
            jnp.transpose(grad_heads.astype(jnp.float32), (1, 0, 2)) * attended, axis=-1
        )
        backward_query_heads = projected[0].reshape(seg_rows, local_heads, head_size)
        bias_zero = jnp.zeros((local_heads, BUCKETS), jnp.float32)
        attend_bias_acc = bias_zero
        bias_acc = attend_bias_acc
        score_scores, score_allowed, score_key_heads = scores_for(
            backward_query_heads,
            lax.all_gather(projected[1], "ctx", axis=0, tiled=True),
            backward_length,
        )
        score_value_heads = lax.all_gather(projected[2], "ctx", axis=0, tiled=True).reshape(
            score_key_heads.shape
        )
        score_key_count = score_key_heads.shape[0]
        soft_weights = jnp.where(
            score_allowed[None], jnp.exp(score_scores - log_total[:, :, None]), 0.0
        )
        weight_grad = jnp.einsum(
            "qhd,khd->hqk", grad_heads, score_value_heads, preferred_element_type=jnp.float32
        )
        score_grad = (soft_weights * (weight_grad - row_delta[:, :, None])).astype(jnp.bfloat16)
        query_acc = jnp.einsum(
            "hqk,khd->qhd", score_grad, score_key_heads, preferred_element_type=jnp.float32
        )
        bias_acc = bias_acc + jnp.dot(
            diagonal_sums(score_grad.astype(jnp.float32)),
            bucket_table(query_first, seg_rows, score_key_count),
            precision=highest,
        )
        (
            (attend_query_acc, attend_bias_acc),
            attend_soft_weights,
            attend_score_grad,
            attend_key_count,
        ) = ((query_acc, bias_acc), soft_weights, score_grad, score_key_count)
        key_term = (
            jnp.einsum(
                "hqk,qhd->khd",
                attend_score_grad,
                backward_query_heads,
                preferred_element_type=jnp.float32,
            )
            * 0.125
        )
        value_term = jnp.einsum(
            "hqk,qhd->khd",
            attend_soft_weights.astype(jnp.bfloat16),
            grad_heads,
            preferred_element_type=jnp.float32,
        )
        grad_term = jnp.stack(
            [key_term.reshape(attend_key_count, -1), value_term.reshape(attend_key_count, -1)],
            axis=1,
        )
        key_value_acc = grad_term
        query_acc, key_value_acc, bias_part = (attend_query_acc, key_value_acc, attend_bias_acc)
        own_grads = lax.psum_scatter(
            key_value_acc.astype(jnp.bfloat16), "ctx", scatter_dimension=0, tiled=True
        ).astype(jnp.float32)
        query_grad = (query_acc * 0.125).reshape(seg_rows, -1).astype(jnp.bfloat16)
        qkv_grad = jnp.stack(
            [
                query_grad,
                own_grads[:, 0].astype(jnp.bfloat16),
                own_grads[:, 1].astype(jnp.bfloat16),
            ],
            axis=0,
        )
        qkv_part = jnp.einsum("td,cte->cde", normed, qkv_grad, preferred_element_type=jnp.float32)
        normed_grad = lax.psum(
            jnp.einsum(
                "cte,cde->td", qkv_grad, qkv_full, preferred_element_type=jnp.float32
            ).astype(jnp.bfloat16),
            "tensor",
        ).astype(jnp.float32)
        unused_first, first_back = jax.vjp(rms_norm, tokens, gain_one.astype(jnp.float32))
        token_grad, gain_one_part = first_back(normed_grad)
        input_part = (token_grad + hidden_grad).astype(jnp.bfloat16)
        weight_parts = (
            gain_one_part,
            qkv_part,
            out_part,
            gain_two_part,
            router_part,
            up_part,
            down_part,
        )
        input_part, weight_parts, bias_part = (input_part, weight_parts, bias_part)
        results.append(result)
        input_parts.append(input_part)
        grad_sums = (
            weight_parts
            if grad_sums is None
            else tuple((old_sum + new_part for old_sum, new_part in zip(grad_sums, weight_parts)))
        )
        bias_total = bias_total + bias_part
    reduced = (
        lax.psum_scatter(grad_sums[0], ("dp", "ctx"), scatter_dimension=0, tiled=True),
        lax.psum_scatter(grad_sums[1], ("dp", "ctx"), scatter_dimension=1, tiled=True),
        lax.psum_scatter(grad_sums[2], ("dp", "ctx"), scatter_dimension=1, tiled=True),
        lax.psum_scatter(grad_sums[3], ("dp", "ctx"), scatter_dimension=0, tiled=True),
        lax.psum_scatter(grad_sums[4], ("dp", "ctx"), scatter_dimension=0, tiled=True),
        lax.psum_scatter(grad_sums[5], ("dp", "ctx"), scatter_dimension=1, tiled=True),
        lax.psum_scatter(grad_sums[6], ("dp", "ctx"), scatter_dimension=2, tiled=True),
    )
    bias_grad_total = lax.psum(bias_total, ("dp", "ctx"))
    return (
        jnp.stack(results, axis=0),
        jnp.stack(input_parts, axis=0),
        reduced[0],
        reduced[1],
        reduced[2],
        jnp.transpose(bias_grad_total),
        reduced[3],
        reduced[4],
        reduced[5],
        reduced[6],
    )


def solution(mesh):
    small = mesh.shape["ctx"] == 2 and mesh.shape["dp"] == 4 and mesh.shape["tensor"] == 4
    return jax.shard_map(
        body_fast if small else body,
        mesh=mesh,
        in_specs=(
            P("dp", "ctx", None),
            P("dp"),
            P("dp", "ctx"),
            P("dp", "ctx", None, None),
            P(("dp", "ctx")),
            P(None, ("dp", "ctx"), "tensor"),
            P("tensor", ("dp", "ctx")),
            P(None, "tensor"),
            P(("dp", "ctx")),
            P(("dp", "ctx"), None),
            P(None, ("dp", "ctx"), "tensor"),
            P(None, "tensor", ("dp", "ctx")),
            P("dp", "ctx", None),
        ),
        out_specs=(
            P("dp", "ctx", None),
            P("dp", "ctx", None),
            P(("dp", "ctx")),
            P(None, ("dp", "ctx"), "tensor"),
            P("tensor", ("dp", "ctx")),
            P(None, "tensor"),
            P(("dp", "ctx")),
            P(("dp", "ctx"), None),
            P(None, ("dp", "ctx"), "tensor"),
            P(None, "tensor", ("dp", "ctx")),
        ),
        check_vma=False,
    )
```

profile of v0, /device:TPU:0, one launch (start us, length us, event | category | flops | bytes accessed | tf_op | source)
XLA Modules:
  0.0 279.3 jit_solution(2035132474948566462)
XLA Ops:
  0.6 0.0 copy-start.3
  0.7 0.0 copy-start.4
  0.7 0.1 pad.11.clone
  0.8 0.8 maximum_maximum_fusion
  1.6 0.2 dynamic_update_slice.3
  1.8 0.9 fusion.1
  2.6 0.1 copy.38
  2.7 0.1 copy.39
  2.9 0.1 copy.33
  3.0 0.1 copy.40
  3.1 0.8 pad_maximum_fusion.4
  4.0 0.1 copy.34
  4.1 0.7 pad_maximum_fusion.2.wsmall
  4.8 0.0 copy-done.3
  4.8 0.0 copy-done.4
  4.8 1.1 pad_maximum_fusion.w
  5.9 262.3 %shard_map.195 = (bf16[1024,768]{1,0:T(8,128)(2,1)}, bf16[1024,768]{1,0:T(8,128)(2,1)}, f32[4,2,96,768]{3,2,1,0:T(8,128)}, f32[96,768]{1,0:T(8,128)}, f32[8,768]...) custom-call(s32[2]{0:T(128)} %len_ref.1, f32[3,32]{1,0:T(4,128)} %bitcast.60, ...), custom_call_target="tpu_custom_call" | custom-call | tf_op jit(solution)/shard_map/pallas_call | solution.py:1053
  268.2 0.0 copy-start
  268.2 1.5 copy.37
  269.7 0.8 constant_dynamic-slice_fusion
  270.5 0.5 slice_bitcast_fusion.3
  271.0 0.6 slice_bitcast_fusion.2
  271.6 1.1 copy.35
  272.7 0.7 fusion
  273.4 0.9 copy.36
  274.3 0.0 copy-done
  274.3 0.0 copy-start.2
  274.3 1.6 slice_bitcast_fusion
  275.9 0.3 copy-done.2
  276.2 1.1 copy.44
  277.4 0.8 copy-done.1
  278.2 1.1 copy.45
  (7 shorter events, 0.1 us)
Async XLA Ops:
  0.6 4.2 %copy-start.3 = (bf16[4,768,96]{1,2,0:T(8,128)(2,1)S(1)}, bf16[4,768,96]{1,2,0:T(8,128)(2,1)}, u32[]{:S(2)}) copy-start(bf16[4,768,96]{1,2,0:T(8,128)(2,1)} %param.23) | copy-start | bytes 1769476
  0.7 4.2 %copy-start.4 = (bf16[4,96,768]{2,1,0:T(8,128)(2,1)S(1)}, bf16[4,96,768]{2,1,0:T(8,128)(2,1)}, u32[]{:S(2)}) copy-start(bf16[4,96,768]{2,1,0:T(8,128)(2,1)} %param.22) | copy-start | bytes 1769476
  268.2 6.1 %copy-start = (f32[4,2,96,768]{3,2,1,0:T(8,128)S(1)}, f32[4,2,96,768]{3,2,1,0:T(8,128)}, u32[]{:S(2)}) copy-start(f32[4,2,96,768]{3,2,1,0:T(8,128)} %get-tuple-element.21) | copy-start | bytes 7077892
  274.3 1.9 copy-start.2
  276.2 2.0 copy-start.1
where the time goes:
time: 280 us; the launch traced here: 279 us
  Pallas kernels  262 us (94%)
  local copies, waits for them, and re-layouts  12.8 us (5%)
  other arithmetic  3.54 us (1%)
    pallas_call x1, Pallas kernels, layer_call(): pl.pallas_call(functools.partial(layer_kernel, heads), out_shape=(sds((ro...  262 us
    unnamed x17, local copies, waits for them, and re-layouts  6.13 us

commit v1 on v0

--- a/solution.py
+++ b/solution.py
@@ -241,15 +241,21 @@
     slot_lanes,
     tok,
     cot,
-    wsmall,
-    w,
+    qkv,
+    out_weight,
+    vectors,
+    up,
+    down_turned,
     result,
     input_grad,
     w_grad,
-    small_grad,
+    qkv_out,
+    out_out,
     tiny_out,
     dbias_out,
     w_full,
+    wsmall,
+    small_grad,
     ws_full,
     ws,
     gains,
@@ -342,14 +348,34 @@
     seg = tok.shape[0] // 2
     width = tok.shape[1]
     shard = width // 8
-    experts = w.shape[0]
+    experts = up.shape[0]
     span = kv.shape[2]
     cap = slot_lanes.shape[2]
+    ahead = low_lanes((shard, 128))
+
+    def packed(base, a, b):
+        turned = jnp.where(ahead, a[:, 0:128], pltpu.roll(b[:, 0:128], 64, 1))
+        wsmall[0:shard, base : base + 128] = turned.astype(BF)
+        turned = jnp.where(ahead, pltpu.roll(a[:, 0:128], 64, 1), b[:, 0:128])
+        wsmall[0:shard, base + 128 : base + 256] = turned.astype(BF)
+        last = jnp.concatenate([a[:, 128:192], b[:, 128:192]], axis=1)
+        wsmall[0:shard, base + 256 : base + 384] = last.astype(BF)
+
+    def unpacked(base):
+        one, two, three = (small_grad[:, base + i * 128 : base + i * 128 + 128] for i in range(3))
+        first = jnp.where(ahead, one, pltpu.roll(two, 64, 1))
+        second = jnp.where(ahead, pltpu.roll(one, 64, 1), two)
+        return first, three[:, 0:64], second, pltpu.roll(three, 64, 1)[:, 0:64]
+
+    packed(0, qkv[1].astype(F32), qkv[2].astype(F32))
+    packed(span, qkv[0].astype(F32), jnp.transpose(out_weight[...].astype(F32)))
+    wsmall[shard:, :] = vectors[...]
     place.greet()
     gather_ring = Ring(place, ag_s, ag_r)
     reduce_ring = Ring(place, rs_s, rs_r)
     sums = TensorSum(place, seg, cbuf, ysend, ybuf, kept, c_s, c_r, y_s, y_r, a_s, a_r)
     bpart = epart
+    earlier = bgrad
 
     def small_slab(k, c):
         return lax.rem(dp + 4 - k, 4) * 2 + c
@@ -363,22 +389,35 @@
         spot = ws_full.at[small_slab(k, c)]
         return remote(wsmall if k == 0 else spot, spot, gx_s.at[k], gx_r.at[k], place.partner)
 
-    small_own = pltpu.make_async_copy(wsmall, ws_full.at[small_slab(0, cx)], local.at[experts])
+    small_own = pltpu.make_async_copy(wsmall, ws_full.at[small_slab(0, cx)], local.at[2 * experts])
 
     def gather(d, e, s, sending):
         away = s - 1 if sending else s
         slab = place.slab(-away if d == 0 else away)
+        if s == 1:
+            spots = [w_full.at[e, j, slab] for j in range(2)]
+            sources = [up.at[e], down_turned.at[e]] if sending else spots
+            return [
+                gather_ring.copy(d, e, at, source, spot)
+                for at, source, spot in zip((1, 5), sources, spots)
+            ]
         spot = w_full.at[e, d, slab] if s == 4 else w_full.at[e, :, slab]
-        return gather_ring.copy(d, e, s, w.at[e] if sending and s == 1 else spot, spot)
+        return [gather_ring.copy(d, e, s, spot, spot)]
 
     def w_own(e):
-        return pltpu.make_async_copy(w.at[e], w_full.at[e, :, place.slab(0)], local.at[e])
+        spots = [w_full.at[e, j, place.slab(0)] for j in range(2)]
+        return [
+            pltpu.make_async_copy(source, spot, local.at[e * 2 + j])
+            for j, (source, spot) in enumerate(zip((up.at[e], down_turned.at[e]), spots))
+        ]
 
     def gather_step(e, s):
         for d in range(2):
             if s > 1:
-                gather(d, e, s - 1, False).wait_recv()
-            gather(d, e, s, True).start()
+                for copy in gather(d, e, s - 1, False):
+                    copy.wait_recv()
+            for copy in gather(d, e, s, True):
+                copy.start()
 
     def landing(d, e, s):
         if s == 1:
@@ -428,12 +467,21 @@
 
         lax.fori_loop(0, shard // 16, add, 0)
 
-    late = [(3, 2), (2, 3), (3, 3), (2, 4), (3, 4)]
+    late = [(1, 4), (3, 2), (2, 3), (3, 3), (2, 4), (3, 4)]
 
     def pump_late(count=1):
         for _ in range(count):
             if late:
                 reduce_step(*late.pop(0))
+
+    def tok_copy(m):
+        rows = sums.own_rows(m)
+        return remote(tok.at[rows], earlier.at[rows], k_s.at[m], k_r.at[m], place.partner)
+
+    @pl.when(cx == 0)
+    def _():
+        for m in range(2):
+            tok_copy(m).start()
 
     small_own.start()
     for k in (1, 3, 2):
@@ -442,12 +490,19 @@
     for e in range(2):
         gather_step(e, 1)
     for e in range(experts):
-        w_own(e).start()
+        for copy in w_own(e):
+            copy.start()
 
     @pl.when(cx == 0)
     def _():
         for m in range(2):
             kv[m, seg:, :] = jnp.zeros((seg, span), BF)
+
+    @pl.when(cx == 1)
+    def _():
+        for m in range(2):
+            tok_copy(m).wait_recv()
+            sums.share(m, 4, earlier)
 
     fill_bias(bias_ref, band, heads)
     spread[...] = jnp.zeros(spread.shape, F32)
@@ -457,6 +512,12 @@
     for k in (1, 3, 2):
         gz_copy(k, small_slab(k, cx)).wait_recv()
         gx_copy(k, cx).start()
+
+    @pl.when(cx == 1)
+    def _():
+        for m in range(2):
+            sums.pass_on(m, 4, earlier)
+
     small_own.wait()
     for k in range(4):
         gx_copy(k, 1 - cx).wait_recv()
@@ -467,38 +528,37 @@
     for i in range(8):
         ws[i * shard : (i + 1) * shard, :] = ws_full[i, 0:shard, :]
 
-    def first_norm(rows):
-        x = tok[rows, :].astype(F32)
+    def first_norm(source, rows):
+        x = source[rows, :].astype(F32)
         scale = lax.rsqrt(jnp.mean(x * x, axis=-1, keepdims=True) + 1e-06)
         return (x * scale * gains[0:1, :]).astype(BF)
 
-    def project(m):
-        def step(i, carry):
-            rows = block(m * seg + i * 256, 256)
-            x = first_norm(rows)
-            kv[m, block(cx * seg + i * 256, 256), :] = mm(x, ws[:, 0:span]).astype(BF)
-            part = mm(x, ws[:, span:])
-            q3[rows, :] = jnp.where(low_lanes(part.shape), part, 0.0).astype(BF)
-            return carry
-
-        lax.fori_loop(0, seg // 256, step, 0)
-
-    def k_copy(m):
-        spot = kv.at[m, block(0, seg), :]
-        return remote(spot, spot, k_s.at[m], k_r.at[m], place.partner)
-
-    for m in range(2):
-        project(m)
-
-        @pl.when(cx == 0)
-        def _():
-            k_copy(m).start()
-
-        if m == 0:
-            gather_step(0, 2)
-        else:
-            gather_step(1, 2)
-            gather_step(2, 1)
+    def project(i, carry):
+        rows = block(i * 256, 256)
+        m, at = lax.div(i, seg // 256), lax.rem(i, seg // 256) * 256
+        x = first_norm(tok, rows)
+        kv[m, block(cx * seg + at, 256), :] = mm(x, ws[:, 0:span]).astype(BF)
+        part = mm(x, ws[:, span:])
+        q3[rows, :] = jnp.where(low_lanes(part.shape), part, 0.0).astype(BF)
+        return carry
+
+    def project_earlier(i, carry):
+        m, at = lax.div(i, seg // 256), lax.rem(i, seg // 256) * 256
+        x = first_norm(earlier, block(i * 256, 256))
+        kv[m, block(at, 256), :] = mm(x, ws[:, 0:span]).astype(BF)
+        return carry
+
+    lax.fori_loop(0, 2 * seg // 256, project, 0)
+    gather_step(0, 2)
+
+    @pl.when(cx == 1)
+    def _():
+        for m in range(2):
+            sums.shared(m, 4, earlier)
+        lax.fori_loop(0, 2 * seg // 256, project_earlier, 0)
+
+    gather_step(1, 2)
+    gather_step(2, 1)
 
     def attend(m):
         length = len_ref[m]
@@ -536,11 +596,6 @@
         sums.share(m, 3, ntwo)
 
     for m in range(2):
-
-        @pl.when(cx == 1)
-        def _():
-            k_copy(m).wait_recv()
-
         attend(m)
         sums.c_copy(m, 3, bpart).start()
         gather_step(m, 3)
@@ -553,6 +608,8 @@
     gather_step(0, 4)
     sums.pass_on(1, 3, ntwo)
     gather_step(1, 4)
+    gather_step(2, 2)
+    gather_step(3, 2)
     for m in range(2):
         sums.shared(m, 3, ntwo)
         sums.c_copy(m, 3, bpart).wait_send()
@@ -606,9 +663,10 @@
         )
 
     def arrived(e):
-        w_own(e).wait()
+        for copy in w_own(e):
+            copy.wait()
         for d in range(2):
-            gather(d, e, 4, False).wait_recv()
+            gather(d, e, 4, False)[0].wait_recv()
         load(e).start()
 
     picked, slot_grad, activated, raised_grad = (ffn.at[i] for i in range(4))
@@ -628,13 +686,8 @@
         return lambda: arrived(e)
 
     before = ([here(0), here(1)], [], [], [])
-    between = ([g(3, 2)], [g(3, 3)], [here(3)], [r(1, 4), start_sums])
-    after = (
-        [g(2, 3)],
-        [g(2, 4), g(3, 4), r(0, 2), here(2), r(1, 2), r(0, 3)],
-        [r(1, 3), r(0, 4)],
-        [r(2, 2)],
-    )
+    between = ([g(2, 3)], [g(2, 4)], [here(3)], [start_sums, r(1, 3)])
+    after = ([g(3, 3)], [g(3, 4), r(0, 2), here(2)], [r(1, 2), r(0, 3)], [r(0, 4), r(2, 2)])
 
     def act_on(e, plan):
         for i, acts in enumerate(plan):
@@ -695,11 +748,16 @@
         act_on(e, after)
         return carry
 
-    gather_step(2, 2)
     lax.fori_loop(0, experts, expert, 0)
 
     for peer in (place.right, place.left):
         pl.semaphore_signal(ready, inc=1, device_id=peer, device_id_type=MESH)
+
+    @pl.when(cx == 1)
+    def _():
+        for m in range(2):
+            for step in range(3):
+                sums.a_copy(m, 4, earlier, step).wait_send()
 
     ones = jnp.ones((8, width), BF)
     for m in range(2):
@@ -722,7 +780,7 @@
 
     for k in (1, 2, 3):
         gg_copy(k).start()
-    pump_late()
+    pump_late(2)
     pl.semaphore_wait(ready, 2)
     for k in (1, 2, 3):
         gg_copy(k).wait_recv()
@@ -813,9 +871,11 @@
 
             grads[pl.ds(m * seg, seg), cut] = dkv_acc[block(cx * seg, seg), :].astype(BF)
 
-            @pl.when(h == 1)
-            def _():
-                pump_late()
+            if m == 1:
+
+                @pl.when(h == 2)
+                def _():
+                    pump_late()
 
             return carry
 
@@ -902,7 +962,7 @@
                 own_result(i)
 
     def normed_again(i, carry):
-        ffn[lax.div(i, 2), block(lax.rem(i, 2) * 256, 256), :] = first_norm(block(i * 256, 256))
+        ffn[lax.div(i, 2), block(lax.rem(i, 2) * 256, 256), :] = first_norm(tok, block(i * 256, 256))
         return carry
 
     lax.fori_loop(0, 2 * seg // 256, normed_again, 0)
@@ -953,7 +1013,7 @@
     tiny_x[2] = tiny_x[0] + tiny_x[1]
     bx_copy.wait_recv()
     dbias_sum = dbias_own[...] + dbias_x[...]
-    dbias_out[...] = dbias_sum
+    dbias_x[...] = dbias_sum
 
     def tz_copy(k):
         return remote(
@@ -962,7 +1022,7 @@
 
     def bz_copy(k):
         return remote(
-            dbias_out, dbias_z.at[k - 1], bz_s.at[k - 1], bz_r.at[k - 1], place.z_peers[k - 1]
+            dbias_x, dbias_z.at[k - 1], bz_s.at[k - 1], bz_r.at[k - 1], place.z_peers[k - 1]
         )
 
     for k in (1, 2, 3):
@@ -977,11 +1037,17 @@
             sz_copy(half, k).wait_recv()
             total = total + sz[half, k - 1].astype(F32)
         small_grad[:, cols] = total
+    first, first_rest, second, second_rest = unpacked(0)
+    qkv_out[1, :, 0:128], qkv_out[1, :, 128:192] = first, first_rest
+    qkv_out[2, :, 0:128], qkv_out[2, :, 128:192] = second, second_rest
+    first, first_rest, second, second_rest = unpacked(span)
+    qkv_out[0, :, 0:128], qkv_out[0, :, 128:192] = first, first_rest
+    out_out[0:128, :], out_out[128:192, :] = jnp.transpose(second), jnp.transpose(second_rest)
     for k in (1, 2, 3):
         bz_copy(k).wait_recv()
         bz_copy(k).wait_send()
         dbias_sum = dbias_sum + dbias_z[k - 1]
-    dbias_out[...] = dbias_sum
+    dbias_out[...] = jnp.transpose(dbias_sum)[0:8, :]
     total = tiny_x[2]
     for k in (1, 2, 3):
         tz_copy(k).wait_recv()
@@ -994,7 +1060,8 @@
     for e in range(experts):
         for d in range(2):
             for s in (1, 2, 3, 4):
-                gather(d, e, s, True).wait_send()
+                for copy in gather(d, e, s, True):
+                    copy.wait_send()
                 reduce_copy(d, e, s).wait_send()
     for k in range(4):
         for half in range(2):
@@ -1023,7 +1090,7 @@
 
         @pl.when(cx == 0)
         def _():
-            k_copy(m).wait_send()
+            tok_copy(m).wait_send()
 
         @pl.when(cx == 1)
         def _():
@@ -1031,11 +1098,11 @@
                 dkv_copy(m, h).wait_send()
 
 
-def layer_call(lengths, bias, slot_lanes, tok, cot, wsmall, w):
+def layer_call(lengths, bias, slot_lanes, tok, cot, qkv, out_weight, vectors, up, down_turned):
     heads = bias.shape[0]
     rows, width = tok.shape
     span = heads * 128
-    experts, ff = w.shape[0], w.shape[3]
+    experts, ff = up.shape[0], up.shape[2]
     seg = rows // 2
     quarter = seg // 4
     shard = width // 8
@@ -1056,15 +1123,18 @@
             sds((rows, width), BF),
             sds((rows, width), BF),
             sds((experts, 2, shard, ff), F32),
-            sds((shard, width), F32),
+            sds(qkv.shape, F32),
+            sds(out_weight.shape, F32),
             sds((8, width), F32),
-            sds((BUCKETS, 128), F32),
+            sds((8, BUCKETS), F32),
             sds((experts, 2, 8, shard, ff), BF),
         ),
-        in_specs=[sm, sm] + [vm] * 3 + [hbm] * 2,
-        out_specs=(hbm,) * 2 + (vm,) * 4 + (hbm,),
+        in_specs=[sm, sm] + [vm] * 6 + [hbm] * 2,
+        out_specs=(hbm,) * 2 + (vm,) * 5 + (hbm,),
         scratch_shapes=[
-            low(8, *wsmall.shape),
+            low(shard + 16, width),
+            full(shard, width),
+            low(8, shard + 16, width),
             low(width, width),
             full(16, width),
             full(2, quarter, width),
@@ -1114,17 +1184,17 @@
             full(3, BUCKETS, 128),
             dma((2,)),
             dma((4,)),
-            dma((experts + 1,)),
+            dma((2 * experts + 1,)),
             pltpu.SemaphoreType.REGULAR,
         ]
         + pair(3)
         + pair(4)
         + pair(2)
-        + pair(2, experts, 4)
+        + pair(2, experts, 5)
         + pair(2, experts, 4)
         + pair(2, 4)
         + pair(2, 4)
-        + pair(2, 4, 3)
+        + pair(2, 5, 3)
         + pair(2, heads)
         + pair(3)
         + pair(2, 4)
@@ -1137,7 +1207,7 @@
         compiler_params=pltpu.CompilerParams(
             collective_id=0, has_side_effects=True, vmem_limit_bytes=63 << 20
         ),
-    )(lengths, bias, slot_lanes, tok, cot, wsmall, w)
+    )(lengths, bias, slot_lanes, tok, cot, qkv, out_weight, vectors, up, down_turned)
 
 
 def body_fast(
@@ -1148,46 +1218,25 @@
     rows = micro * seg
     experts = up_weight.shape[0]
     heads = position_bias.shape[1]
-    size = qkv_weight.shape[2] // heads
     slab = lax.axis_index("dp") * 2 + lax.axis_index("ctx")
     shard = attn_gain.shape[0]
-    by_head = jnp.concatenate(
-        [
-            qkv_weight[1].reshape(shard, heads, 1, size),
-            qkv_weight[2].reshape(shard, heads, 1, size),
-        ],
-        axis=2,
-    ).reshape(shard, -1)
-    by_query = jnp.concatenate(
-        [
-            qkv_weight[0].reshape(shard, heads, 1, size),
-            out_weight.T.reshape(shard, heads, 1, size),
-        ],
-        axis=2,
-    ).reshape(shard, -1)
     small = jnp.concatenate(
         [attn_gain[None], ffn_gain[None], router_weight.T, jnp.zeros((10, shard), BF)], axis=0
     )
     small = lax.dynamic_update_slice(jnp.zeros((16, width), BF), small, (0, slab * shard))
-    wsmall = jnp.concatenate([jnp.concatenate([by_head, by_query], axis=1), small], axis=0)
-    w = jnp.stack([up_weight, jnp.transpose(down_weight, (0, 2, 1))], axis=1)
-    tok = inputs.reshape(rows, width)
-    result, input_part, w_grad, small_grad, tiny, dbias, _ = layer_call(
-        lengths, position_bias.T, slot_rows.reshape(micro, experts, -1), tok,
-        cotangent.reshape(rows, width), wsmall, w,
+    result, input_part, w_grad, qkv_grad, out_grad, tiny, dbias, _ = layer_call(
+        lengths, position_bias.T, slot_rows.reshape(micro, experts, -1), inputs.reshape(rows, width),
+        cotangent.reshape(rows, width), qkv_weight, out_weight, small, up_weight,
+        jnp.transpose(down_weight, (0, 2, 1)),
     )
     tiny = lax.dynamic_slice_in_dim(tiny, slab * shard, shard, axis=1)
-    parts = small_grad.reshape(shard, 2, heads, 2, size)
-    qkv_grad = jnp.stack(
-        [parts[:, 1, :, 0], parts[:, 0, :, 0], parts[:, 0, :, 1]], axis=0
-    ).reshape(3, shard, heads * size)
     return (
         result.reshape(inputs.shape),
         input_part.reshape(inputs.shape),
         tiny[0],
         qkv_grad,
-        parts[:, 1, :, 1].reshape(shard, heads * size).T,
-        dbias[:, :heads],
+        out_grad,
+        dbias[:heads].T,
         tiny[1],
         tiny[2 : 2 + experts].T,
         w_grad[:, 0],

time: 280 us -> 266 us (0.950)
  Pallas kernels: 262 us -> 253 us
    pallas_call x1, Pallas kernels: 262 us -> 253 us  [layer_call(): pl.pallas_call(functools.partial(layer_kernel, heads), out_shape=(sds((ro...]
    unnamed x17 -> x14, local copies, waits for them, and re-layouts: 6.13 us -> 5.09 us
where the time goes in v1:
time: 266 us
  Pallas kernels  253 us (95%)
  local copies, waits for them, and re-layouts  11.7 us (4%)
    pallas_call x1, Pallas kernels, layer_call(): pl.pallas_call(functools.partial(layer_kernel, heads), out_shape=(sds((ro...  253 us

profile of v1, /device:TPU:0, one launch (start us, length us, event | category | flops | bytes accessed | tf_op | source)
XLA Modules:
  0.0 266.0 jit_solution(8497367223932623121)
XLA Ops:
  0.7 0.1 pad.3.clone
  0.7 0.8 maximum_maximum_fusion
  1.5 0.2 dynamic_update_slice.3.vectors
  1.7 0.0 copy-start.3
  1.7 0.6 copy-done.3
  2.3 252.8 %shard_map.195 = (bf16[1024,768]{1,0:T(8,128)(2,1)}, bf16[1024,768]{1,0:T(8,128)(2,1)}, f32[4,2,96,768]{3,2,1,0:T(8,128)}, f32[3,96,192]{2,1,0:T(8,128)}, f32[19...) custom-call(s32[2]{0:T(128)} %len_ref.1, f32[3,32]{1,0:T(4,128)} %bitcast.30, ...), custom_call_target="tpu_custom_call" | custom-call | tf_op jit(solution)/shard_map/pallas_call | solution.py:1120
  255.1 1.3 slice_bitcast_fusion.3
  256.3 0.8 constant_dynamic-slice_fusion
  257.1 0.5 slice_bitcast_fusion.4
  257.6 0.6 slice_bitcast_fusion.2
  258.2 0.0 copy-start.1
  258.2 3.3 %slice_bitcast_fusion = (f32[4,768,96]{1,2,0:T(8,128)}, f32[4,96,768]{2,1,0:T(8,128)}) fusion(f32[4,2,96,768]{3,2,1,0:T(8,128)} %get-tuple-element.23), kind=kLoop, calls=%fused_computation | loop fusion | bytes 4718592 | tf_op jit(solution)/shard_map/transpose | solution.py:1243
  261.5 0.0 copy-done.1
  261.5 0.0 copy-start
  261.5 1.1 copy.27
  262.6 0.8 copy-done
  263.5 0.0 copy-start.2
  263.5 0.0 copy-start.4
  263.5 1.1 copy.28
  264.6 0.0 copy-done.2
  264.6 0.7 copy.29
  265.3 0.0 copy-done.4
  265.3 0.6 copy.30
  (2 shorter events, 0.0 us)
Async XLA Ops:
  1.7 0.6 copy-start.3
  258.2 3.3 %copy-start.1 = (bf16[1024,768]{1,0:T(8,128)(2,1)S(1)}, bf16[1024,768]{1,0:T(8,128)(2,1)}, u32[]{:S(2)}) copy-start(bf16[1024,768]{1,0:T(8,128)(2,1)} %get-tuple-element.17) | copy-start | bytes 4718596
  261.5 2.0 copy-start
  263.5 1.1 copy-start.2
  263.5 1.9 copy-start.4

commit v2 on v1

--- a/solution.py
+++ b/solution.py
@@ -248,7 +248,8 @@
     down_turned,
     result,
     input_grad,
-    w_grad,
+    up_out,
+    down_out,
     qkv_out,
     out_out,
     tiny_out,
@@ -462,7 +463,8 @@
             total = gw[e, :, place.slab(0), rows, :].astype(F32)
             for d in range(2):
                 total = total + landing(d, e, 4)[:, rows, :].astype(F32)
-            w_grad[e, :, rows, :] = total
+            up_out[e, rows, :] = total[0]
+            down_out[e, rows, :] = total[1]
             return carry
 
         lax.fori_loop(0, shard // 16, add, 0)
@@ -602,14 +604,14 @@
         if m == 1:
             second_norm(0)
         sums.to_quarters(m, 3, bpart)
-    gather_step(3, 1)
+    gather_step(2, 2)
     second_norm(1)
     sums.pass_on(0, 3, ntwo)
     gather_step(0, 4)
     sums.pass_on(1, 3, ntwo)
     gather_step(1, 4)
-    gather_step(2, 2)
-    gather_step(3, 2)
+    gather_step(3, 1)
+    gather_step(2, 3)
     for m in range(2):
         sums.shared(m, 3, ntwo)
         sums.c_copy(m, 3, bpart).wait_send()
@@ -686,8 +688,13 @@
         return lambda: arrived(e)
 
     before = ([here(0), here(1)], [], [], [])
-    between = ([g(2, 3)], [g(2, 4)], [here(3)], [start_sums, r(1, 3)])
-    after = ([g(3, 3)], [g(3, 4), r(0, 2), here(2)], [r(1, 2), r(0, 3)], [r(0, 4), r(2, 2)])
+    between = ([g(3, 2)], [g(3, 3), g(3, 4)], [], [start_sums, r(1, 3)])
+    after = (
+        [g(2, 4)],
+        [here(2), r(0, 2)],
+        [here(3), r(1, 2), r(0, 3)],
+        [r(0, 4), r(2, 2)],
+    )
 
     def act_on(e, plan):
         for i, acts in enumerate(plan):
@@ -814,10 +821,7 @@
         tiny_own[1:2, :] += jnp.sum(gain_terms, axis=0, keepdims=True)
         tiny_own[...] += mm_tn(logit_grad, ntwo[rows, :])[0:8, :]
     pump_late()
-    for m in range(2):
-        sums.pass_on(m, 0, bgrad)
-    for m in range(2):
-        sums.to_quarters(m, 0, epart)
+    sums.pass_on(0, 0, bgrad)
 
     def dkv_copy(m, h):
         spot = dkv.at[m, h]
@@ -947,6 +951,10 @@
         sums.shared(m, 0, bgrad)
         attend_back(m)
         if m == 0:
+            sums.pass_on(1, 0, bgrad)
+            for i in range(2):
+                sums.to_quarters(i, 0, epart)
+        if m == 1:
             for i in range(2):
 
                 def own_result(i):
@@ -969,6 +977,9 @@
     for k in range(4):
         gx_copy(k, cx).wait_send()
     small_part(1)
+    bucket_sums(heads, band_sum, whole_sum, dbias_own)
+    bx_copy = remote(dbias_own, dbias_x, bx_s.at[0], bx_r.at[0], place.partner)
+    bx_copy.start()
     sums.c_copy(0, 1, npart).wait_send()
     sums.y_copy(0, 1).wait_send()
     after_attend(0)
@@ -997,38 +1008,39 @@
     for k in (1, 2, 3):
         tt_copy(k).start()
     small_step(1)
+    bx_copy.wait_recv()
+    dbias_sum = dbias_own[...] + dbias_x[...]
+    dbias_x[...] = dbias_sum
+
+    def bz_copy(k):
+        return remote(
+            dbias_x, dbias_z.at[k - 1], bz_s.at[k - 1], bz_r.at[k - 1], place.z_peers[k - 1]
+        )
+
+    for k in (1, 2, 3):
+        bz_copy(k).start()
+    reduce_end(0)
+    reduce_end(1)
     small_step(0)
     for k in (1, 2, 3):
         tt_copy(k).wait_recv()
     tiny_x[0] = tiny_own[...] + tiny_t[0] + tiny_t[1] + tiny_t[2]
     tx_copy = remote(tiny_x.at[0], tiny_x.at[1], tx_s.at[0], tx_r.at[0], place.partner)
     tx_copy.start()
-    bucket_sums(heads, band_sum, whole_sum, dbias_own)
-    bx_copy = remote(dbias_own, dbias_x, bx_s.at[0], bx_r.at[0], place.partner)
-    bx_copy.start()
     for m in range(2):
         sums.pass_on(m, 1, result)
         sums.pass_on(m, 2, input_grad)
     tx_copy.wait_recv()
     tiny_x[2] = tiny_x[0] + tiny_x[1]
-    bx_copy.wait_recv()
-    dbias_sum = dbias_own[...] + dbias_x[...]
-    dbias_x[...] = dbias_sum
 
     def tz_copy(k):
         return remote(
             tiny_x.at[2], tiny_z.at[k - 1], tz_s.at[k - 1], tz_r.at[k - 1], place.z_peers[k - 1]
         )
 
-    def bz_copy(k):
-        return remote(
-            dbias_x, dbias_z.at[k - 1], bz_s.at[k - 1], bz_r.at[k - 1], place.z_peers[k - 1]
-        )
-
     for k in (1, 2, 3):
         tz_copy(k).start()
-        bz_copy(k).start()
-    for e in range(experts):
+    for e in range(2, experts):
         reduce_end(e)
     for half in range(2):
         cols = slice(half * span, (half + 1) * span)
@@ -1047,12 +1059,13 @@
         bz_copy(k).wait_recv()
         bz_copy(k).wait_send()
         dbias_sum = dbias_sum + dbias_z[k - 1]
-    dbias_out[...] = jnp.transpose(dbias_sum)[0:8, :]
+    dbias_out[...] = jnp.transpose(dbias_sum)[0:heads, :]
     total = tiny_x[2]
     for k in (1, 2, 3):
         tz_copy(k).wait_recv()
         total = total + tiny_z[k - 1]
-    tiny_out[...] = total
+    turn = lax.rem(width - (dp * 2 + cx) * shard, width)
+    tiny_out[...] = pltpu.roll(total, turn, 1)[:, 0:shard]
     for m in range(2):
         sums.shared(m, 1, result)
         sums.shared(m, 2, input_grad)
@@ -1122,15 +1135,16 @@
         out_shape=(
             sds((rows, width), BF),
             sds((rows, width), BF),
-            sds((experts, 2, shard, ff), F32),
+            sds((experts, shard, ff), F32),
+            sds((experts, shard, ff), F32),
             sds(qkv.shape, F32),
             sds(out_weight.shape, F32),
-            sds((8, width), F32),
-            sds((8, BUCKETS), F32),
+            sds((8, shard), F32),
+            sds((heads, BUCKETS), F32),
             sds((experts, 2, 8, shard, ff), BF),
         ),
         in_specs=[sm, sm] + [vm] * 6 + [hbm] * 2,
-        out_specs=(hbm,) * 2 + (vm,) * 5 + (hbm,),
+        out_specs=(hbm,) * 2 + (vm,) * 6 + (hbm,),
         scratch_shapes=[
             low(shard + 16, width),
             full(shard, width),
@@ -1217,30 +1231,28 @@
     micro, seg, width = inputs.shape
     rows = micro * seg
     experts = up_weight.shape[0]
-    heads = position_bias.shape[1]
     slab = lax.axis_index("dp") * 2 + lax.axis_index("ctx")
     shard = attn_gain.shape[0]
     small = jnp.concatenate(
         [attn_gain[None], ffn_gain[None], router_weight.T, jnp.zeros((10, shard), BF)], axis=0
     )
     small = lax.dynamic_update_slice(jnp.zeros((16, width), BF), small, (0, slab * shard))
-    result, input_part, w_grad, qkv_grad, out_grad, tiny, dbias, _ = layer_call(
+    result, input_part, up_grad, down_grad, qkv_grad, out_grad, tiny, dbias, _ = layer_call(
         lengths, position_bias.T, slot_rows.reshape(micro, experts, -1), inputs.reshape(rows, width),
         cotangent.reshape(rows, width), qkv_weight, out_weight, small, up_weight,
         jnp.transpose(down_weight, (0, 2, 1)),
     )
-    tiny = lax.dynamic_slice_in_dim(tiny, slab * shard, shard, axis=1)
     return (
         result.reshape(inputs.shape),
         input_part.reshape(inputs.shape),
         tiny[0],
         qkv_grad,
         out_grad,
-        dbias[:heads].T,
+        dbias.T,
         tiny[1],
         tiny[2 : 2 + experts].T,
-        w_grad[:, 0],
-        jnp.transpose(w_grad[:, 1], (0, 2, 1)),
+        up_grad,
+        jnp.transpose(down_grad, (0, 2, 1)),
     )
 
 

time: 266 us -> 266 us (level)
    transpose x2 -> x0, local copies, waits for them, and re-layouts: 4.55 us -> none  [the longest x1 3.3 us: body_fast(): jnp.transpose(w_grad[:, 1], (0, 2, 1))]
    unnamed x14 -> x21, local copies, waits for them, and re-layouts: 5.09 us -> 8.5 us
where the time goes in v2:
time: 266 us; the launch traced here: 265 us
  Pallas kernels  253 us (95%)
  local copies, waits for them, and re-layouts  11.3 us (4%)
    pallas_call x1, Pallas kernels, layer_call(): pl.pallas_call(functools.partial(layer_kernel, heads), out_shape=(sds((ro...  253 us
    unnamed x21, local copies, waits for them, and re-layouts  8.5 us

profile of v2, /device:TPU:0, one launch (start us, length us, event | category | flops | bytes accessed | tf_op | source)
XLA Modules:
  0.0 265.3 jit_solution(1506347001465549259)
XLA Ops:
  0.7 0.1 pad.3.clone
  0.7 0.8 maximum_maximum_fusion
  1.5 0.2 dynamic_update_slice.3.vectors
  1.7 0.0 copy-start.4
  1.7 0.6 copy-done.4
  2.3 252.6 %shard_map.195 = (bf16[1024,768]{1,0:T(8,128)(2,1)}, bf16[1024,768]{1,0:T(8,128)(2,1)}, f32[4,96,768]{2,1,0:T(8,128)}, f32[4,96,768]{2,1,0:T(8,128)}, f32[3,96,1...) custom-call(s32[2]{0:T(128)} %len_ref.1, ...), custom_call_target="tpu_custom_call" | custom-call | tf_op jit(solution)/shard_map/pallas_call | solution.py:1133
  254.9 1.3 slice_bitcast_fusion.1
  256.2 1.3 slice_bitcast_fusion
  257.4 0.0 copy-start
  257.4 2.8 %copy.30 = bf16[2,512,768]{2,1,0:T(8,128)(2,1)} copy(bf16[2,512,768]{2,1,0:T(8,128)(2,1)} %bitcast.21) | data formatting | bytes 3145728
  260.2 0.0 copy-done
  260.2 0.0 copy-start.3
  260.2 0.0 copy-start.5
  260.2 0.0 copy-start.6
  260.2 0.0 copy-start.2
  260.2 1.1 copy.31
  261.4 0.0 copy-done.3
  261.4 0.0 copy-start.1
  261.4 0.7 copy.32
  262.1 0.0 copy-done.5
  262.1 0.6 copy.33
  262.7 0.0 copy-done.6
  262.7 0.6 copy.34
  263.3 0.0 copy-done.2
  263.3 1.0 copy.35
  264.3 0.0 copy-done.1
  264.3 1.0 copy.36
  (2 shorter events, 0.0 us)
Async XLA Ops:
  1.7 0.6 copy-start.4
  257.4 2.8 %copy-start = (bf16[1024,768]{1,0:T(8,128)(2,1)S(1)}, bf16[1024,768]{1,0:T(8,128)(2,1)}, u32[]{:S(2)}) copy-start(bf16[1024,768]{1,0:T(8,128)(2,1)} %get-tuple-element.19) | copy-start | bytes 4718596
  260.2 1.2 copy-start.3
  260.2 1.9 copy-start.5
  260.2 2.5 copy-start.6
  260.2 3.1 %copy-start.2 = (f32[4,96,768]{2,1,0:T(8,128)S(1)}, f32[4,96,768]{2,1,0:T(8,128)}, u32[]{:S(2)}) copy-start(f32[4,96,768]{2,1,0:T(8,128)} %get-tuple-element.46) | copy-start | bytes 3538948
  261.4 3.0 %copy-start.1 = (f32[4,96,768]{2,1,0:T(8,128)S(1)}, f32[4,96,768]{2,1,0:T(8,128)}, u32[]{:S(2)}) copy-start(f32[4,96,768]{2,1,0:T(8,128)} %get-tuple-element.25) | copy-start | bytes 3538948
